TPU v7x, 512 devices: a whole 4x8x8 slice. The times are simulated.
512 devices in a mesh: cell: 8 (over z), donor: 8 (over x, core), gene: 8 (over y).
Axes of the slice: x: 4, y: 8, z: 8, core: 2. Of those that a mesh axis runs over, the one named last changes fastest.
Arguments:
- counts: int32 [32768, 2048], P(('cell', 'donor'), 'gene'), may hold values from 0 to 35
- cell_donor: int32 [32768], P(('cell', 'donor')), may hold values from 0 to 511, as said below
- cell_type: int32 [32768], P(('cell', 'donor')), may hold values from -1 to 23, as said below
- covariates: float32 [512, 50], P(('cell', 'donor')), may hold values from -6 to 6
- dosage: int32 [8192, 512], P('gene'), may hold values from 0 to 2
- windows: int32 [2048, 1024], P(('gene', 'cell', 'donor')), may hold values from -1 to 8191, as said below
Outputs:
- association: float32 [24, 2048, 1024], P(None, ('gene', 'cell', 'donor'))
Inputs may be any that keep to these rules, and one draw needn't show every extreme that they name: `cell_donor`: rows come in blocks of 512: a row of block b names a donor d with (d // 8) % 8 = b % 8. Every donor has at least one cell of every cell type. `cell_type`: in each block of 512 rows the live slots (type 0 or more) come first and the empty ones (-1) last; the number of live slots varies from block to block and some block is full. `windows`: row j lists consecutive SNP numbers in ascending order, then -1 to its end; all of them lie in [b * 1024, (b + 1) * 1024) with b = j // 256. A window holds 512 to 1024 SNPs, some window holds exactly 1024, and the last gene's window ends at the last SNP.
All inputs are finite; a program needn't handle non-finite values.
Results may differ from a plain program's by a relative error of at most 0.00045.
Values sent between devices are 32-bit elements; how exact they have to be, the bound alone decides.
No kernel may reach another device: no remote copies, remote signals or barrier semaphores. Data moves between devices by JAX's collectives and lax.ppermute only.
A program may use at most 64 MiB of HBM per device.

v0:
```python
import math

import jax
import jax.numpy as jnp
from jax import lax
from jax.sharding import PartitionSpec as P

CT = 24


def log_cpm(pseudobulk, library):
    return jnp.log2((pseudobulk + 0.5) / (library + 1.0) * 1000000.0)


def with_intercept(covariates):
    intercept = jnp.ones((covariates.shape[0], 1), jnp.float32)
    return jnp.concatenate([intercept, covariates], axis=1)


def factor_lower(gram_sum):
    order = gram_sum.shape[0]
    factor = jnp.zeros_like(gram_sum)
    for column in range(order):
        known = factor[column, :column]
        pivot = jnp.sqrt(gram_sum[column, column] - jnp.sum(known * known))
        factor = factor.at[column, column].set(pivot)
        if column + 1 < order:
            below = gram_sum[column + 1 :, column] - jnp.dot(
                factor[column + 1 :, :column], known, precision=lax.Precision.HIGHEST
            )
            factor = factor.at[column + 1 :, column].set(below / pivot)
    return factor


def solve_written(factor, right_rows):
    order = factor.shape[0]
    forward = []
    for row in range(order):
        value = right_rows[row]
        if row > 0:
            value = value - jnp.dot(
                factor[row, :row], jnp.stack(forward), precision=lax.Precision.HIGHEST
            )
        forward.append(value / factor[row, row])
    backward = [None] * order
    for row in range(order - 1, -1, -1):
        value = forward[row]
        if row < order - 1:
            later = jnp.stack(backward[row + 1 :])
            value = value - jnp.dot(factor[row + 1 :, row], later, precision=lax.Precision.HIGHEST)
        backward[row] = value / factor[row, row]
    return jnp.stack(backward)


def solve_normal(gram_sum, cross_sum):
    order = gram_sum.shape[0]
    factor = factor_lower(gram_sum)
    inverse = solve_written(factor, jnp.eye(order, dtype=jnp.float32))
    return jnp.einsum("kj,cjg->ckg", inverse, cross_sum, precision=lax.Precision.HIGHEST)


def association_block(residual, dosage, windows, first_snp):
    window_len = windows.shape[1]
    every_snp = jnp.einsum(
        "sd,dcg->gsc", dosage.astype(jnp.float32), residual, precision=lax.Precision.HIGHEST
    )
    padded = jnp.pad(every_snp, ((0, 0), (0, window_len), (0, 0)))
    starts = windows[:, 0] - first_snp
    gene_ids = jnp.arange(windows.shape[0], dtype=jnp.int32)

    def one_gene(pair):
        gene_id, start = pair
        gene_rows = lax.dynamic_index_in_dim(padded, gene_id, 0, keepdims=False)
        return lax.dynamic_slice_in_dim(gene_rows, start, window_len, 0)

    sliced = lax.map(one_gene, (gene_ids, starts))
    products = jnp.transpose(sliced, (2, 0, 1))
    scaling = 1.0 / math.sqrt(dosage.shape[1])
    return jnp.where((windows >= 0)[None], products, 0.0) * scaling


def owner_index(cell_donor, cell_type, donors_here, groups):
    cell_slot = cell_donor // (donors_here * groups)
    local_donor = cell_slot * donors_here + cell_donor % donors_here
    return jnp.where(cell_type >= 0, local_donor * CT + cell_type, -1)


def per_device(counts, cell_donor, cell_type, covariates, dosage, windows):
    groups = lax.axis_size("donor")
    donors_here = covariates.shape[0]
    cell_count = counts.shape[0]
    owner_slot = owner_index(cell_donor, cell_type, donors_here, groups)
    counts_half = counts.astype(jnp.bfloat16)
    first_snp = lax.axis_index("gene") * dosage.shape[0]
    row_ids = lax.broadcasted_iota(
        jnp.int32, (donors_here * CT * lax.axis_size("cell"), cell_count), 0
    )
    onehot_table = (row_ids == owner_slot[None, :]).astype(jnp.bfloat16)
    pseudobulk = lax.psum_scatter(
        jnp.dot(onehot_table, counts_half, preferred_element_type=jnp.float32),
        "cell",
        scatter_dimension=0,
        tiled=True,
    )
    library = lax.psum(jnp.sum(pseudobulk, axis=1), "gene")
    expression = log_cpm(pseudobulk, library[:, None]).reshape(donors_here, CT, -1)
    design = with_intercept(covariates)
    gram_part = jnp.dot(design.T, design, precision=lax.Precision.HIGHEST)
    cross_part = jnp.einsum("dk,dcg->ckg", design, expression, precision=lax.Precision.HIGHEST)
    gram_sum, cross_sum = lax.psum((gram_part, cross_part), ("cell", "donor"))
    coefficients = solve_normal(gram_sum, cross_sum)
    residual = expression - jnp.einsum(
        "dk,ckg->dcg", design, coefficients, precision=lax.Precision.HIGHEST
    )
    regrouped = lax.all_to_all(residual, ("cell", "donor"), split_axis=2, concat_axis=0, tiled=True)
    return association_block(regrouped, dosage, windows, first_snp)


def solution(mesh):
    in_specs = (
        P(("cell", "donor"), "gene"),
        P(("cell", "donor")),
        P(("cell", "donor")),
        P(("cell", "donor"), None),
        P("gene", None),
        P(("gene", "cell", "donor"), None),
    )
    out_specs = P(None, ("gene", "cell", "donor"), None)
    return jax.shard_map(
        per_device, mesh=mesh, in_specs=in_specs, out_specs=out_specs, check_vma=False
    )
```

profile of v0, /device:TPU:1, one launch (start us, length us, event | category | flops | bytes accessed | tf_op | source)
XLA Modules:
  0.0 813.1 jit_solution(3078640551746485459)
XLA Ops:
  7.3 2.8 fusion
  10.5 252.7 %psum.23 = f32[51,51]{1,0:T(8,128)S(1)} all-reduce(f32[51,51]{1,0:T(8,128)S(1)} %fusion.449), channel_id=1, replica_groups=mesh['cell'=8,'donor'=8,'gene'=8] {'cell','donor'}, use_global_device_ids=true, to_apply=%region_4.5 | all-reduce | flops 2601 | bytes 20808 | tf_op jit(solution)/shard_map/psum | solution.py:110
  375.8 11.7 %scatter.456 = f32[51,51]{1,0:T(8,128)S(1)} dynamic-update-slice(f32[51,51]{1,0:T(8,128)S(1)} %copy.362, f32[1,1]{1,0:T(1,128)} %bitcast.220, s32[]{:T(128)} %constant.2846.clone.1, s32[]{:T(128)} %constant.2846.clone.1) | dynamic-update-slice | bytes 12 | tf_op jit(solution)/shard_map/scatter | solution.py:26
  431.1 1.8 fusion.481
  497.7 0.8 fusion.295
  510.8 0.8 fusion.321
  517.2 1.0 reduce_sum.454
  518.2 14.1 %psum.21 = f32[192]{0:T(256)S(1)} all-reduce(f32[192]{0:T(256)S(1)} %reduce_sum.454), channel_id=1, replica_groups=mesh['cell'=8,'donor'=8,'gene'=8] {'gene'}, use_global_device_ids=true, to_apply=%region_2.3 | all-reduce | flops 192 | bytes 1536 | tf_op jit(solution)/shard_map/psum | solution.py:105
  532.3 1.0 log_multiply_fusion
  533.3 2.5 convolution_bitcast_fusion.1
  537.1 1.4 fusion.335
  539.7 193.4 %all-reduce.5.cloned.1.call-done = f32[24,51,256]{2,1,0:T(8,128)} async-done(((f32[24,51,256]{2,1,0:T(8,128)}), f32[24,51,256]{2,1,0:T(8,128)}) %all-reduce.5.cloned.1.call-update) | async-done | bytes 1253392 | tf_op jit(solution)/shard_map/psum | solution.py:110
  733.0 2.6 convolution_bitcast_fusion
  736.9 1.5 reshape.3475
  738.4 9.8 %all-to-all-start = ((f32[64,1,768]{2,1,0:T(1,128)}), f32[64,1,768]{2,1,0:T(1,128)S(1)}, u32[]{:S(2)}, u32[]{:S(2)}) async-start(f32[64,1,768]{2,1,0:T(1,128)} %reshape.3475), calls=%async_computation.1 | async-start | bytes 393216 | tf_op jit(solution)/shard_map/all_to_all | solution.py:115
  748.3 11.7 %all-to-all-done = f32[64,1,768]{2,1,0:T(1,128)S(1)} async-done(((f32[64,1,768]{2,1,0:T(1,128)}), f32[64,1,768]{2,1,0:T(1,128)S(1)}, u32[]{:S(2)}, u32[]{:S(2)}) %all-to-all-start) | async-done | bytes 196640 | tf_op jit(solution)/shard_map/all_to_all | solution.py:115
  760.6 1.2 reduce.398
  762.6 6.8 fusion.5
  769.4 34.5 %while.115 = (s32[]{:T(128)}, f32[4,1024,24]{1,0,2:T(4,128)}, s32[4]{0:T(128)S(1)}, s32[4]{0:T(128)S(1)}, f32[4,2048,24]{1,2,0:T(8,128)S(1)}) while((s32[]{:T(128)}, f32[4,1024,24]{1,0,2:T(4,128)}, s32[4]{0:T(128)S(1)}, s32[4]{0:T(128)S(1)}, f32[4,2048,24]{1,2,0:T(8,128)S(1)}) %tuple.543), condition=%wide.region_55.56_spmd.clone, body=%wide.region_54.55_spmd.sunk.clone | while | flops 10 | bytes 590021 | solution.py:76
  775.1 2.9 dynamic_update_slice.10
  783.8 2.9 dynamic_update_slice.10
  792.4 2.9 dynamic_update_slice.10
  801.0 2.9 dynamic_update_slice.10
  803.9 1.9 multiply_bitcast_fusion
  (625 shorter events, 181.2 us)
Async XLA Ops:
  6.5 510.6 %reduce-scatter.2.cloned.1.call-start = ((), (), s32[]{:S(2)}) async-start(), calls=%async_computation.2 | async-start | bytes 1769472 | tf_op jit(solution)/shard_map/reduce_scatter | solution.py:99
  7.2 2.9 copy-start.1
  10.1 722.9 %all-reduce.5.cloned.1.call-start = ((), (), s32[]{:S(2)}) async-start(), calls=%async_computation.3 | async-start | bytes 2752512 | tf_op jit(solution)/shard_map/psum | solution.py:110
  736.4 11.7 %copy-start.2 = (s32[4,1024]{1,0:T(4,128)S(1)}, s32[4,1024]{1,0:T(4,128)}, u32[]{:S(2)}) copy-start(s32[4,1024]{1,0:T(4,128)} %param.215) | copy-start | bytes 49156
  736.9 25.7 %copy-start = (s32[1024,512]{1,0:T(8,128)S(1)}, s32[1024,512]{1,0:T(8,128)}, u32[]{:S(2)}) copy-start(s32[1024,512]{1,0:T(8,128)} %param.214) | copy-start | bytes 6291460
  738.4 21.7 %all-to-all-start = ((f32[64,1,768]{2,1,0:T(1,128)}), f32[64,1,768]{2,1,0:T(1,128)S(1)}, u32[]{:S(2)}, u32[]{:S(2)}) async-start(f32[64,1,768]{2,1,0:T(1,128)} %reshape.3475), calls=%async_computation.1 | async-start | bytes 393216 | tf_op jit(solution)/shard_map/all_to_all | solution.py:115
Sparse Core Ops, SparseCore 0:
  10.3 45.2 reduce-scatter.1
  535.9 197.0 all-reduce.4
where the time goes:
time: 824 us; the launch traced here: 813 us
  blocking collectives  267 us (32%)
  waiting for transfers between devices  205 us (25%)
  matrix products  96.3 us (12%)
  local copies, waits for them, and re-layouts  94.6 us (11%)
  between operations  84 us (10%)
  other arithmetic  39.8 us (5%)
  loops' own time  16.7 us (2%)
  starting transfers between devices  9.82 us (1%)
    psum x1, blocking collectives, per_device(): gram_sum, cross_sum = lax.psum((gram_part, cross_part), ('cell', 'donor'))  253 us
    psum x1, waiting for transfers between devices, per_device(): gram_sum, cross_sum = lax.psum((gram_part, cross_part), ('cell', 'donor'))  193 us
    dot_general x49, matrix products, solve_written(): jnp.dot(factor[row + 1:, row], later, precision=lax.Precision.HIGHEST)  37.7 us
    dot_general x49, matrix products, solve_written(): jnp.dot(factor[row, :row], jnp.stack(forward), precision=lax.Precision.HI...  36.4 us
    reduce_sum x49, other arithmetic, factor_lower(): pivot = jnp.sqrt(gram_sum[column, column] - jnp.sum(known * known))  30 us
    scatter x50, local copies, waits for them, and re-layouts, factor_lower(): factor = factor.at[column + 1:, column].set(below / pivot)  19.3 us
    scatter x50, local copies, waits for them, and re-layouts, factor_lower(): factor = factor.at[column, column].set(pivot)  18.7 us
    another operation x1, loops' own time, association_block(): sliced = lax.map(one_gene, (gene_ids, starts))  16.7 us
  transfers between devices with their start and end apart: 3, of which 2 were waited for; matrix products, arithmetic and copies ran while one was open for 23% of the time, Pallas kernels for 0%

commit v1 on v0

v1 whole, which is shorter than its diff:
```python
import math

import jax
import jax.numpy as jnp
from jax import lax
from jax.experimental import pallas as pl
from jax.experimental.pallas import tpu as pltpu
from jax.sharding import PartitionSpec as P

F32 = jnp.float32
BF16 = jnp.bfloat16
I32 = jnp.int32
HIGHEST = lax.Precision.HIGHEST

CT = 24
HALF = CT // 2
NCOV = 50
ORDER = NCOV + 1
N = 8
CELLS = 512
LANES = 128
CHUNKS = CELLS // LANES
GENES = 256
GENE_PART = GENES // N
OWN = GENE_PART // N
DON_GRP = 64
DONORS = N * DON_GRP
SNPS = 1024
WIN = 1024
LABEL_ROW = CHUNKS * GENE_PART
PART_ROWS = LABEL_ROW + 2 * CHUNKS
SUM_ROWS = HALF * GENE_PART
LIB_ROWS = 16

NT = (((1,), (1,)), ((), ()))


def split3(value):
    high = value.astype(BF16)
    rest = value - high.astype(F32)
    middle = rest.astype(BF16)
    low = (rest - middle.astype(F32)).astype(BF16)
    return high, middle, low


def pack_kernel(counts_ref, donor_ref, type_ref, part_ref, total_ref):
    donor = donor_ref[...].astype(F32)
    kind = type_ref[...].astype(F32)
    labels = jnp.concatenate([donor, kind], axis=0)
    totals = []
    for chunk in range(CHUNKS):
        rows = counts_ref[chunk * LANES : (chunk + 1) * LANES, :].astype(F32)
        turned = rows.T
        totals.append(jnp.sum(turned, axis=0, keepdims=True))
        for peer in range(N):
            part_ref[peer, chunk * GENE_PART : (chunk + 1) * GENE_PART, :] = turned[
                peer * GENE_PART : (peer + 1) * GENE_PART
            ]
    for peer in range(N):
        part_ref[peer, LABEL_ROW:PART_ROWS, :] = labels
    total = jnp.concatenate(totals, axis=0)
    total_ref[...] = jnp.broadcast_to(total[None], total_ref.shape)


def to_row(block):
    return jnp.concatenate([block[row : row + 1] for row in range(CHUNKS)], axis=1)


def expression_kernel(part_ref, total_ref, out_ref, sum_ref):
    sum_ref[...] = jnp.zeros_like(sum_ref)

    def one_block(block, carry):
        labels = part_ref[block, LABEL_ROW:PART_ROWS, :]
        donor = to_row(labels[:CHUNKS]).astype(I32)
        kind = to_row(labels[CHUNKS:]).astype(I32)
        local = ((donor >> 6) << 3) + (donor & 7)
        upper = kind >= HALF
        column = jnp.where(kind >= 0, jnp.where(upper, local + DON_GRP, local), -1)
        step = jnp.where(upper, kind - HALF, kind)
        place = lax.broadcasted_iota(I32, (LANES, CELLS), 0)
        onehot = jnp.where(place == column, 1.0, 0.0).astype(BF16)
        counts = jnp.concatenate(
            [
                part_ref[block, chunk * GENE_PART : (chunk + 1) * GENE_PART, :]
                for chunk in range(CHUNKS)
            ],
            axis=1,
        )
        step_full = jnp.broadcast_to(step, (GENE_PART, CELLS))
        pieces = [
            jnp.where(step_full == number, counts, 0.0).astype(BF16) for number in range(HALF)
        ]
        total = total_ref[block * N]
        for gene in range(1, N):
            total = total + total_ref[block * N + gene]
        total = to_row(total)
        number = lax.broadcasted_iota(I32, (LIB_ROWS, CELLS), 0)
        wanted = number == step
        for piece in split3(total):
            pieces.append(jnp.where(wanted, piece.astype(F32), 0.0).astype(BF16))
        left = jnp.concatenate(pieces, axis=0)
        sum_ref[...] += lax.dot_general(left, onehot, NT, preferred_element_type=F32)
        return carry

    lax.fori_loop(0, N, one_block, 0)
    library = (
        sum_ref[SUM_ROWS : SUM_ROWS + LIB_ROWS]
        + sum_ref[SUM_ROWS + LIB_ROWS : SUM_ROWS + 2 * LIB_ROWS]
        + sum_ref[SUM_ROWS + 2 * LIB_ROWS : SUM_ROWS + 3 * LIB_ROWS]
    )
    for step in range(HALF):
        summed = sum_ref[step * GENE_PART : (step + 1) * GENE_PART, :]
        expression = jnp.log2((summed + 0.5) / (library[step : step + 1] + 1.0) * 1000000.0)
        for peer in range(N):
            out_ref[peer, step * OWN : (step + 1) * OWN, :] = expression[
                peer * OWN : (peer + 1) * OWN
            ]


def projection_kernel(cov_ref, dosage_ref, high_ref, middle_ref, low_ref, dosage_out_ref):
    dosage_out_ref[...] = dosage_ref[...].astype(F32).astype(BF16)
    lane = lax.broadcasted_iota(I32, (DONORS, LANES), 1)
    natural = jnp.where(lane == NCOV, 1.0, cov_ref[...].reshape(DONORS, LANES))
    grouped = jnp.concatenate(
        [cov_ref[cell * N + donor] for donor in range(N) for cell in range(N)], axis=0
    )
    grouped = jnp.where(lane == NCOV, 1.0, grouped)
    turned = natural.T
    gram = lax.dot_general(turned, turned, NT, precision=HIGHEST, preferred_element_type=F32)
    rows = 56
    row_id = lax.broadcasted_iota(I32, (rows, LANES), 0)
    lane_id = lax.broadcasted_iota(I32, (rows, LANES), 1)
    work = jnp.where(lane_id < 64, gram[:rows], jnp.where(lane_id - 64 == row_id, 1.0, 0.0))
    row_col = lax.broadcasted_iota(I32, (rows, 1), 0)
    for column in range(ORDER):
        pivot_row = work[column : column + 1, :]
        scaled = pivot_row / pivot_row[:, column : column + 1]
        below = jnp.where(row_col > column, work[:, column : column + 1], 0.0)
        work = work - below * scaled
    pivots = jnp.sum(jnp.where(lane_id == row_id, work, 0.0), axis=1, keepdims=True)
    scale = 1.0 / jnp.sqrt(jnp.where(row_col < ORDER, pivots, 1.0))
    inverse = pltpu.roll(work, 64, 1)
    inverse = jnp.where((lane_id < ORDER) & (row_id < ORDER), inverse * scale, 0.0)
    left = lax.dot_general(grouped, inverse, NT, precision=HIGHEST, preferred_element_type=F32)
    right = lax.dot_general(
        inverse, turned, (((1,), (0,)), ((), ())), precision=HIGHEST, preferred_element_type=F32
    )
    span = 128
    for start in range(0, DONORS, span):
        row = lax.broadcasted_iota(I32, (span, DONORS), 0) + start
        column = lax.broadcasted_iota(I32, (span, DONORS), 1)
        same = (((row >> 3) & 7) << 6) + ((row >> 6) << 3) + (row & 7) == column
        fitted = lax.dot_general(
            left[start : start + span],
            right,
            (((1,), (0,)), ((), ())),
            precision=HIGHEST,
            preferred_element_type=F32,
        )
        kept = jnp.where(same, 1.0, 0.0) - fitted
        high, middle, low = split3(kept)
        high_ref[start : start + span, :] = high
        middle_ref[start : start + span, :] = middle
        low_ref[start : start + span, :] = low


def association_kernel(
    expr_ref, high_ref, middle_ref, low_ref, dosage_ref, windows_ref, first_ref, out_ref
):
    rows = HALF * OWN
    lane = lax.broadcasted_iota(I32, (rows, LANES), 1)
    lower, upper = [], []
    for pair in range(N // 2):
        one, two = expr_ref[2 * pair], expr_ref[2 * pair + 1]
        lower.append(jnp.where(lane < 64, one, pltpu.roll(two, 64, 1)))
        upper.append(jnp.where(lane < 64, pltpu.roll(one, 64, 1), two))
    expression = jnp.concatenate(
        [jnp.concatenate(lower, axis=1), jnp.concatenate(upper, axis=1)], axis=0
    )
    both = 2 * rows
    parts = jnp.concatenate(split3(expression), axis=0)
    plain = (((1,), (0,)), ((), ()))
    first = lax.dot_general(parts, high_ref[...], plain, preferred_element_type=F32)
    second = lax.dot_general(parts[: 2 * both], middle_ref[...], plain, preferred_element_type=F32)
    third = lax.dot_general(parts[:both], low_ref[...], plain, preferred_element_type=F32)
    residual = (
        (third + second[both:] + first[2 * both :]) + (second[:both] + first[both : 2 * both])
    ) + first[:both]
    upper_part = residual.astype(BF16)
    lower_part = (residual - upper_part.astype(F32)).astype(BF16)
    products = lax.dot_general(
        jnp.concatenate([upper_part, lower_part], axis=0),
        dosage_ref[...],
        NT,
        preferred_element_type=F32,
    )
    products = (products[:both] + products[both:]) * (1.0 / math.sqrt(DONORS))
    gene_of_row = lax.broadcasted_iota(I32, (both, WIN), 0) & (OWN - 1)
    windows = windows_ref[...]
    result = jnp.zeros_like(products)
    for gene in range(OWN):
        start = first_ref[gene] & (SNPS - 1)
        turned = pltpu.roll(products, (SNPS - start) & (SNPS - 1), 1)
        live = windows[gene : gene + 1] >= 0
        result = jnp.where((gene_of_row == gene) & live, turned, result)
    for kind in range(CT):
        out_ref[kind] = result[kind * OWN : (kind + 1) * OWN]


VMEM = pl.BlockSpec(memory_space=pltpu.VMEM)
SMEM = pl.BlockSpec(memory_space=pltpu.SMEM)
PARAMS = pltpu.CompilerParams(vmem_limit_bytes=48 * 1024 * 1024)


def call(kernel, name, outs, n_in, scratch=(), smem_last=False):
    specs = [VMEM] * n_in
    if smem_last:
        specs[-1] = SMEM
    return pl.pallas_call(
        kernel,
        name=name,
        out_shape=outs,
        in_specs=specs,
        out_specs=jax.tree.map(lambda _: VMEM, outs),
        scratch_shapes=scratch,
        compiler_params=PARAMS,
    )


def shape(*dims, dtype=F32):
    return jax.ShapeDtypeStruct(dims, dtype)


pack = call(pack_kernel, "pack", [shape(N, PART_ROWS, LANES), shape(N * N, CHUNKS, LANES)], 3)
express = call(
    expression_kernel,
    "express",
    shape(N, HALF * OWN, LANES),
    2,
    [pltpu.VMEM((SUM_ROWS + 3 * LIB_ROWS, LANES), F32)],
)
project = call(
    projection_kernel,
    "project",
    [shape(DONORS, DONORS, dtype=BF16)] * 3 + [shape(SNPS, DONORS, dtype=BF16)],
    2,
)
associate = call(
    association_kernel, "associate", shape(CT, OWN, WIN), 7, smem_last=True
)


def per_device(counts, cell_donor, cell_type, covariates, dosage, windows):
    parts, totals = pack(
        counts, cell_donor.reshape(CHUNKS, LANES), cell_type.reshape(CHUNKS, LANES)
    )
    parts = lax.all_to_all(parts, "cell", 0, 0, tiled=True)
    totals = lax.all_to_all(totals, ("cell", "gene"), 0, 0, tiled=True)
    padded = jnp.pad(covariates, ((0, 0), (0, LANES - NCOV)))
    every = lax.all_to_all(
        jnp.broadcast_to(padded[None], (N * N,) + padded.shape),
        ("cell", "donor"),
        0,
        0,
        tiled=True,
    )
    high, middle, low, dosage_half = project(every, dosage)
    expression = express(parts, totals)
    expression = lax.all_to_all(expression, "donor", 0, 0, tiled=True)
    return associate(expression, high, middle, low, dosage_half, windows, windows[:, 0])


def solution(mesh):
    in_specs = (
        P(("cell", "donor"), "gene"),
        P(("cell", "donor")),
        P(("cell", "donor")),
        P(("cell", "donor"), None),
        P("gene", None),
        P(("gene", "cell", "donor"), None),
    )
    out_specs = P(None, ("gene", "cell", "donor"), None)
    return jax.shard_map(
        per_device, mesh=mesh, in_specs=in_specs, out_specs=out_specs, check_vma=False
    )
```

time: 824 us -> 93.3 us (0.11); the launches traced: 813 us -> 92.7 us
  blocking collectives: 267 us -> 28.5 us
  waiting for transfers between devices: 205 us -> 25.7 us
  matrix products: 96.3 us -> 0 us
  local copies, waits for them, and re-layouts: 94.6 us -> 10 us
  between operations: 84 us -> 0.05 us
  other arithmetic: 39.8 us -> 0 us
  loops' own time: 16.7 us -> 0 us
  Pallas kernels: 0 us -> 13.7 us
    psum x2 -> x0, blocking collectives: 267 us -> none  [the longest x1 253 us: per_device(): gram_sum, cross_sum = lax.psum((gram_part, cross_part), ('cell', 'donor'))]
    psum x1 -> x0, waiting for transfers between devices: 193 us -> none  [per_device(): gram_sum, cross_sum = lax.psum((gram_part, cross_part), ('cell', 'donor'))]
    dot_general x151 -> x0, matrix products: 96.3 us -> none  [the longest x49 37.7 us: solve_written(): jnp.dot(factor[row + 1:, row], later, precision=lax.Precision.HIGHEST)]
    scatter x100 -> x0, local copies, waits for them, and re-layouts: 38 us -> none  [the longest x50 19.3 us: factor_lower(): factor = factor.at[column + 1:, column].set(below / pivot)]
    reduce_sum x50 -> x0, other arithmetic: 31 us -> none  [the longest x49 30 us: factor_lower(): pivot = jnp.sqrt(gram_sum[column, column] - jnp.sum(known * known))]
    all_to_all x0 -> x1, blocking collectives: none -> 28.5 us  [per_device(): totals = lax.all_to_all(totals, ('cell', 'gene'), 0, 0, tiled=True)]
    slice x103 -> x1, local copies, waits for them, and re-layouts: 22 us -> 0.11 us  [per_device(): windows[:, 0]]
    another operation x1 -> x0, loops' own time: 16.7 us -> none  [association_block(): sliced = lax.map(one_gene, (gene_ids, starts))]
  transfers between devices with their start and end apart: 3 -> 3, of which waited for: 2 -> 2; matrix products, arithmetic and copies ran while one was open for 23% -> 1% of each run, Pallas kernels for 0% -> 11%
where the time goes in v1:
time: 93.3 us; the launch traced here: 92.7 us
  blocking collectives  28.5 us (31%)
  waiting for transfers between devices  25.7 us (28%)
  starting transfers between devices  14.7 us (16%)
  Pallas kernels  13.7 us (15%)
  local copies, waits for them, and re-layouts  10 us (11%)
    all_to_all x1, blocking collectives, per_device(): totals = lax.all_to_all(totals, ('cell', 'gene'), 0, 0, tiled=True)  28.5 us
    all_to_all x1, waiting for transfers between devices, per_device(): parts = lax.all_to_all(parts, 'cell', 0, 0, tiled=True)  15.6 us
    all_to_all x1, waiting for transfers between devices, per_device(): lax.all_to_all(jnp.broadcast_to(padded[None], (N * N,) + padded.shape), (...  10.1 us
    unnamed x22, local copies, waits for them, and re-layouts  8.48 us
    all_to_all x1, starting transfers between devices, per_device(): lax.all_to_all(jnp.broadcast_to(padded[None], (N * N,) + padded.shape), (...  7.61 us
    pallas_call x1, Pallas kernels, per_device(): high, middle, low, dosage_half = project(every, dosage)  6.78 us
    all_to_all x1, starting transfers between devices, per_device(): expression = lax.all_to_all(expression, 'donor', 0, 0, tiled=True)  3.58 us
    all_to_all x1, starting transfers between devices, per_device(): parts = lax.all_to_all(parts, 'cell', 0, 0, tiled=True)  3.54 us
  transfers between devices with their start and end apart: 3, of which 2 were waited for; matrix products, arithmetic and copies ran while one was open for 1% of the time, Pallas kernels for 11%

profile of v1, /device:TPU:1, one launch (start us, length us, event | category | flops | bytes accessed | tf_op | source)
XLA Modules:
  0.0 92.7 jit_solution(18230092006616361619)
XLA Ops:
  0.0 1.2 %copy-done.3 = s32[512,256]{1,0:T(8,128)S(1)} copy-done((s32[512,256]{1,0:T(8,128)S(1)}, s32[512,256]{1,0:T(8,128)}, u32[]{:S(2)}) %copy-start.3) | copy-done | bytes 524312
  1.2 0.7 copy-done.9
  1.9 0.7 copy-done.10
  2.6 1.0 %pack.1 = (f32[8,136,128]{2,1,0:T(8,128)}, f32[64,4,128]{2,1,0:T(4,128)S(1)}) custom-call(s32[512,256]{1,0:T(8,128)S(1)} %copy-done.3, s32[4,128]{1,0:T(4,128)S(1)} %bitcast.2, s32[4,128]{1,0:T(4,128)S(1)} %bitcast.3), custom_call_target="tpu_custom_call" | custom-call | tf_op jit(solution)/shard_map/pack/pallas_call | solution.py:254
  3.6 28.5 %all_to_all.20.total_ref = f32[64,4,128]{2,1,0:T(4,128)S(1)} all-to-all(f32[64,4,128]{2,1,0:T(4,128)S(1)} %get-tuple-element.12), channel_id=1, replica_groups=mesh['cell'=8,'donor'=8,'gene'=8] {'cell','gene'}, dimensions={0} | all-to-all | bytes 262144 | tf_op jit(solution)/shard_map/all_to_all | solution.py:258
  32.0 3.5 %all-to-all-start = ((f32[8,136,128]{2,1,0:T(8,128)}), f32[8,136,128]{2,1,0:T(8,128)S(1)}, u32[]{:S(2)}, u32[]{:S(2)}) async-start(f32[8,136,128]{2,1,0:T(8,128)} %get-tuple-element.11), calls=%async_computation | async-start | bytes 1114112 | tf_op jit(solution)/shard_map/all_to_all | solution.py:257
  35.6 0.7 pad.4
  36.3 15.6 %all-to-all-done.part_ref = f32[8,136,128]{2,1,0:T(8,128)S(1)} async-done(((f32[8,136,128]{2,1,0:T(8,128)}), f32[8,136,128]{2,1,0:T(8,128)S(1)}, u32[]{:S(2)}, u32[]{:S(2)}) %all-to-all-start) | async-done | bytes 557088 | tf_op jit(solution)/shard_map/all_to_all | solution.py:257
  51.9 0.7 broadcast_in_dim.2
  52.6 7.6 %all-to-all-start.3 = ((f32[64,8,128]{2,1,0:T(8,128)}), f32[64,8,128]{2,1,0:T(8,128)S(1)}, u32[]{:S(2)}, u32[]{:S(2)}) async-start(f32[64,8,128]{2,1,0:T(8,128)} %broadcast_in_dim.2), calls=%async_computation.3 | async-start | bytes 524288 | tf_op jit(solution)/shard_map/all_to_all | solution.py:260
  60.2 3.1 %express.1 = f32[8,48,128]{2,1,0:T(8,128)} custom-call(f32[8,136,128]{2,1,0:T(8,128)S(1)} %all-to-all-done.part_ref, f32[64,4,128]{2,1,0:T(4,128)S(1)} %all_to_all.20.total_ref), custom_call_target="tpu_custom_call" | custom-call | tf_op jit(solution)/shard_map/express/pallas_call | solution.py:268
  63.3 10.1 %all-to-all-done.3.cov_ref = f32[64,8,128]{2,1,0:T(8,128)S(1)} async-done(((f32[64,8,128]{2,1,0:T(8,128)}), f32[64,8,128]{2,1,0:T(8,128)S(1)}, u32[]{:S(2)}, u32[]{:S(2)}) %all-to-all-start.3) | async-done | bytes 262176 | tf_op jit(solution)/shard_map/all_to_all | solution.py:260
  73.4 3.6 %all-to-all-start.2 = ((f32[8,48,128]{2,1,0:T(8,128)}), f32[8,48,128]{2,1,0:T(8,128)S(1)}, u32[]{:S(2)}, u32[]{:S(2)}) async-start(f32[8,48,128]{2,1,0:T(8,128)} %express.1), calls=%async_computation.2 | async-start | bytes 393216 | tf_op jit(solution)/shard_map/all_to_all | solution.py:269
  77.0 0.1 slice_reduce_fusion.first_ref
  77.1 0.0 copy-done
  77.1 6.8 %project.1 = (bf16[512,512]{1,0:T(8,128)(2,1)S(1)}, bf16[512,512]{1,0:T(8,128)(2,1)S(1)}, bf16[512,512]{1,0:T(8,128)(2,1)S(1)}, bf16[1024,512]{1,0:T(8,128)(2,1)S(1)}) custom-call(f32[64,8,128]{2,1,0:T(8,128)S(1)} %all-to-all-done.3.cov_ref, s32[1024,512]{1,0:T(8,128)S(1)} %copy-done), custom_call_target="tpu_custom_call" | custom-call | tf_op jit(solution)/shard_map/project/pallas_call | solution.py:267
  83.9 1.0 %copy-done.1 = bf16[1024,512]{1,0:T(8,128)(2,1)} copy-done((bf16[1024,512]{1,0:T(8,128)(2,1)}, bf16[1024,512]{1,0:T(8,128)(2,1)S(1)}, u32[]{:S(2)}) %copy-start.1) | copy-done | bytes 1048600
  84.9 0.8 copy-done.4
  85.7 0.8 copy-done.6
  86.5 0.0 all-to-all-done.2.expr_ref
  86.5 1.2 %copy-done.2 = bf16[1024,512]{1,0:T(8,128)(2,1)S(1)} copy-done((bf16[1024,512]{1,0:T(8,128)(2,1)S(1)}, bf16[1024,512]{1,0:T(8,128)(2,1)}, u32[]{:S(2)}) %copy-start.2) | copy-done | bytes 1048600
  87.8 1.0 %copy-done.5 = bf16[512,512]{1,0:T(8,128)(2,1)S(1)} copy-done((bf16[512,512]{1,0:T(8,128)(2,1)S(1)}, bf16[512,512]{1,0:T(8,128)(2,1)}, u32[]{:S(2)}) %copy-start.5) | copy-done | bytes 524312
  88.8 1.0 %copy-done.7 = bf16[512,512]{1,0:T(8,128)(2,1)S(1)} copy-done((bf16[512,512]{1,0:T(8,128)(2,1)S(1)}, bf16[512,512]{1,0:T(8,128)(2,1)}, u32[]{:S(2)}) %copy-start.7) | copy-done | bytes 524312
  89.8 2.9 %associate.1 = f32[24,4,1024]{2,1,0:T(4,128)} custom-call(f32[8,48,128]{2,1,0:T(8,128)S(1)} %all-to-all-done.2.expr_ref, bf16[512,512]{1,0:T(8,128)(2,1)S(1)} %get-tuple-element.13.high_ref, bf16[512,512]{1,0:T(8,128)(2,1)S(1)} %copy-done.5, bf16[512,512]{1,0:T(8,128)(2,1)S(1)} %copy-done.7, bf16[1024,512]{1,0:T(8,128)(2,1)S(1)} %copy-done.2, ...), custom_call_target="tpu_custom_call" | custom-call | tf_op jit(solution)/shard_map/associate/pallas_call | solution.py:270
  (12 shorter events, 0.0 us)
Async XLA Ops:
  0.0 77.1 %copy-start = (s32[1024,512]{1,0:T(8,128)S(1)}, s32[1024,512]{1,0:T(8,128)}, u32[]{:S(2)}) copy-start(s32[1024,512]{1,0:T(8,128)} %dosage_ref.1) | copy-start | bytes 6291460
  0.0 1.2 %copy-start.3 = (s32[512,256]{1,0:T(8,128)S(1)}, s32[512,256]{1,0:T(8,128)}, u32[]{:S(2)}) copy-start(s32[512,256]{1,0:T(8,128)} %counts_ref.1) | copy-start | bytes 1572868
  1.2 0.7 copy-start.9
  1.9 0.7 copy-start.10
  2.6 74.4 %copy-start.8 = (s32[4,1024]{1,0:T(4,128)S(1)}, s32[4,1024]{1,0:T(4,128)}, u32[]{:S(2)}) copy-start(s32[4,1024]{1,0:T(4,128)} %windows_ref.1) | copy-start | bytes 49156
  32.0 19.9 %all-to-all-start = ((f32[8,136,128]{2,1,0:T(8,128)}), f32[8,136,128]{2,1,0:T(8,128)S(1)}, u32[]{:S(2)}, u32[]{:S(2)}) async-start(f32[8,136,128]{2,1,0:T(8,128)} %get-tuple-element.11), calls=%async_computation | async-start | bytes 1114112 | tf_op jit(solution)/shard_map/all_to_all | solution.py:257
  52.6 20.8 %all-to-all-start.3 = ((f32[64,8,128]{2,1,0:T(8,128)}), f32[64,8,128]{2,1,0:T(8,128)S(1)}, u32[]{:S(2)}, u32[]{:S(2)}) async-start(f32[64,8,128]{2,1,0:T(8,128)} %broadcast_in_dim.2), calls=%async_computation.3 | async-start | bytes 524288 | tf_op jit(solution)/shard_map/all_to_all | solution.py:260
  73.4 13.1 %all-to-all-start.2 = ((f32[8,48,128]{2,1,0:T(8,128)}), f32[8,48,128]{2,1,0:T(8,128)S(1)}, u32[]{:S(2)}, u32[]{:S(2)}) async-start(f32[8,48,128]{2,1,0:T(8,128)} %express.1), calls=%async_computation.2 | async-start | bytes 393216 | tf_op jit(solution)/shard_map/all_to_all | solution.py:269
  83.9 1.0 %copy-start.1 = (bf16[1024,512]{1,0:T(8,128)(2,1)}, bf16[1024,512]{1,0:T(8,128)(2,1)S(1)}, u32[]{:S(2)}) copy-start(bf16[1024,512]{1,0:T(8,128)(2,1)S(1)} %get-tuple-element.16.dosage_ref) | copy-start | bytes 3145732
  84.9 0.8 copy-start.4
  85.7 0.8 copy-start.6
  86.5 1.2 %copy-start.2 = (bf16[1024,512]{1,0:T(8,128)(2,1)S(1)}, bf16[1024,512]{1,0:T(8,128)(2,1)}, u32[]{:S(2)}) copy-start(bf16[1024,512]{1,0:T(8,128)(2,1)} %copy-done.1) | copy-start | bytes 3145732
  87.7 1.0 %copy-start.5 = (bf16[512,512]{1,0:T(8,128)(2,1)S(1)}, bf16[512,512]{1,0:T(8,128)(2,1)}, u32[]{:S(2)}) copy-start(bf16[512,512]{1,0:T(8,128)(2,1)} %copy-done.4) | copy-start | bytes 1572868
  88.8 1.0 %copy-start.7 = (bf16[512,512]{1,0:T(8,128)(2,1)S(1)}, bf16[512,512]{1,0:T(8,128)(2,1)}, u32[]{:S(2)}) copy-start(bf16[512,512]{1,0:T(8,128)(2,1)} %copy-done.6) | copy-start | bytes 1572868

commit v2 on v1

v2 whole, which is shorter than its diff:
```python
import math

import jax
import jax.numpy as jnp
from jax import lax
from jax.experimental import pallas as pl
from jax.experimental.pallas import tpu as pltpu
from jax.sharding import PartitionSpec as P

F32 = jnp.float32
BF16 = jnp.bfloat16
I32 = jnp.int32
HIGHEST = lax.Precision.HIGHEST

CT = 24
SUB = 8
PARTS = CT // SUB
NCOV = 50
ORDER = NCOV + 1
N = 8
PEERS = N * N
CELLS = 512
LANES = 128
CHUNKS = CELLS // LANES
GENES = 256
OWN = GENES // PEERS
DON_GRP = 64
DONORS = N * DON_GRP
SNPS = 1024
WIN = 1024
ROWS = 32
DONOR_ROW = CHUNKS * OWN
TYPE_ROW = DONOR_ROW + CHUNKS
TOTAL_ROW = TYPE_ROW + CHUNKS
COV_ROW = TOTAL_ROW + CHUNKS
KINDS = OWN + 2

NT = (((1,), (1,)), ((), ()))


def split3(value):
    high = value.astype(BF16)
    rest = value - high.astype(F32)
    middle = rest.astype(BF16)
    low = (rest - middle.astype(F32)).astype(BF16)
    return high, middle, low


def pack_kernel(
    counts_hbm, donor_hbm, type_hbm, cov_hbm, part_ref,
    counts_ref, donor_ref, type_ref, cov_ref, wide_ref, sems,
):
    copies = [
        pltpu.make_async_copy(
            counts_hbm.at[pl.ds(chunk * LANES, LANES)],
            counts_ref.at[pl.ds(chunk * LANES, LANES)],
            sems.at[chunk],
        )
        for chunk in range(CHUNKS)
    ]
    copies.append(pltpu.make_async_copy(donor_hbm, donor_ref, sems.at[CHUNKS]))
    copies.append(pltpu.make_async_copy(type_hbm, type_ref, sems.at[CHUNKS + 1]))
    copies.append(pltpu.make_async_copy(cov_hbm, cov_ref, sems.at[CHUNKS + 2]))
    for copy in copies:
        copy.start()
    totals = []
    for chunk in range(CHUNKS):
        copies[chunk].wait()
        turned = counts_ref[chunk * LANES : (chunk + 1) * LANES, :].astype(F32).T
        totals.append(jnp.sum(turned, axis=0, keepdims=True))
        for peer in range(PEERS):
            part_ref[peer, chunk * OWN : (chunk + 1) * OWN, :] = turned[
                peer * OWN : (peer + 1) * OWN
            ]
    for copy in copies[CHUNKS:]:
        copy.wait()
    wide_ref[...] = jnp.zeros_like(wide_ref)
    wide_ref[:, :NCOV] = cov_ref[...]
    wide = wide_ref[...]
    paired = wide[: N // 2] + pltpu.roll(wide, DON_GRP, 1)[N // 2 :]
    shared = jnp.concatenate(
        [donor_ref[...].astype(F32), type_ref[...].astype(F32), *totals, paired], axis=0
    )
    for peer in range(PEERS):
        part_ref[peer, DONOR_ROW:ROWS, :] = shared


def to_row(block):
    return jnp.concatenate([block[row : row + 1] for row in range(CHUNKS)], axis=1)


def sum_kernel(part_ref, sum_ref, library_ref):
    lane = lax.broadcasted_iota(I32, (KINDS * SUB, LANES), 1)

    def one_block(block):
        block_rows = part_ref[block]
        donor = to_row(block_rows[DONOR_ROW:TYPE_ROW]).astype(I32)
        kind = to_row(block_rows[TYPE_ROW:TOTAL_ROW]).astype(I32)
        local = ((donor >> 6) << 3) + (donor & 7)
        column = jnp.where(kind >= 0, ((kind >> 3) << 6) + local, -1)
        place = lax.broadcasted_iota(I32, (PARTS * DON_GRP, CELLS), 0)
        onehot = jnp.where(place == column, 1.0, 0.0).astype(BF16)
        wanted = lax.broadcasted_iota(I32, (SUB, CELLS), 0) == (kind & 7)
        total = to_row(block_rows[TOTAL_ROW:COV_ROW])
        high = total.astype(BF16).astype(F32)
        values = [
            jnp.concatenate(
                [
                    block_rows[chunk * OWN + gene : chunk * OWN + gene + 1]
                    for chunk in range(CHUNKS)
                ],
                axis=1,
            )
            for gene in range(OWN)
        ]
        values += [high, total - high]
        left = jnp.concatenate([jnp.where(wanted, value, 0.0) for value in values], axis=0)
        return lax.dot_general(left.astype(BF16), onehot, NT, preferred_element_type=F32)

    def one_pair(pair, carry):
        even, odd = one_block(2 * pair), one_block(2 * pair + 1)
        for cell in range(1, N):
            even = even + one_block(cell * N + 2 * pair)
            odd = odd + one_block(cell * N + 2 * pair + 1)
        even_low, odd_low = even[:, :LANES], odd[:, :LANES]
        merged = [
            jnp.where(lane < DON_GRP, even_low, pltpu.roll(odd_low, DON_GRP, 1)),
            jnp.where(lane < DON_GRP, pltpu.roll(even_low, DON_GRP, 1), odd_low),
            jnp.concatenate([even[:, LANES:], odd[:, LANES:]], axis=1),
        ]
        span = pl.ds(pl.multiple_of(pair * LANES, LANES), LANES)
        for part, value in enumerate(merged):
            for gene in range(OWN):
                start = gene * CT + part * SUB
                sum_ref[start : start + SUB, span] = value[gene * SUB : (gene + 1) * SUB]
            library = value[OWN * SUB : (OWN + 1) * SUB] + value[(OWN + 1) * SUB :]
            for peer in range(N):
                library_ref[peer, part * SUB : (part + 1) * SUB, span] = library
        return carry

    lax.fori_loop(0, N // 2, one_pair, 0)


def projection_kernel(part_ref, dosage_ref, high_ref, middle_ref, low_ref, dosage_out_ref):
    dosage_out_ref[...] = dosage_ref[...].astype(F32).astype(BF16)
    lane = lax.broadcasted_iota(I32, (SUB, LANES), 1)
    first_half = lax.broadcasted_iota(I32, (SUB, LANES), 0) < N // 2
    tiles = []
    for block in range(PEERS):
        tile = part_ref[block, TOTAL_ROW:ROWS, :]
        rows = jnp.where(first_half, pltpu.roll(tile, N // 2, 0), pltpu.roll(tile, DON_GRP, 1))
        tiles.append(jnp.where(lane < NCOV, rows, jnp.where(lane == NCOV, 1.0, 0.0)))
    natural = jnp.concatenate(tiles, axis=0)
    grouped = jnp.concatenate(
        [tiles[cell * N + donor] for donor in range(N) for cell in range(N)], axis=0
    )
    turned = natural.T
    gram = lax.dot_general(turned, turned, NT, precision=HIGHEST, preferred_element_type=F32)
    rows = 56
    row_id = lax.broadcasted_iota(I32, (rows, LANES), 0)
    lane_id = lax.broadcasted_iota(I32, (rows, LANES), 1)
    work = jnp.where(lane_id < 64, gram[:rows], jnp.where(lane_id - 64 == row_id, 1.0, 0.0))
    row_col = lax.broadcasted_iota(I32, (rows, 1), 0)
    for column in range(ORDER):
        pivot_row = work[column : column + 1, :]
        scaled = pivot_row / pivot_row[:, column : column + 1]
        below = jnp.where(row_col > column, work[:, column : column + 1], 0.0)
        work = work - below * scaled
    pivots = jnp.sum(jnp.where(lane_id == row_id, work, 0.0), axis=1, keepdims=True)
    scale = 1.0 / jnp.sqrt(jnp.where(row_col < ORDER, pivots, 1.0))
    inverse = pltpu.roll(work, 64, 1)
    inverse = jnp.where((lane_id < ORDER) & (row_id < ORDER), inverse * scale, 0.0)
    left = lax.dot_general(grouped, inverse, NT, precision=HIGHEST, preferred_element_type=F32)
    right = lax.dot_general(
        inverse, turned, (((1,), (0,)), ((), ())), precision=HIGHEST, preferred_element_type=F32
    )
    span = 128
    for start in range(0, DONORS, span):
        row = lax.broadcasted_iota(I32, (span, DONORS), 0) + start
        column = lax.broadcasted_iota(I32, (span, DONORS), 1)
        same = (((row >> 3) & 7) << 6) + ((row >> 6) << 3) + (row & 7) == column
        fitted = lax.dot_general(
            left[start : start + span],
            right,
            (((1,), (0,)), ((), ())),
            precision=HIGHEST,
            preferred_element_type=F32,
        )
        kept = jnp.where(same, 1.0, 0.0) - fitted
        high, middle, low = split3(kept)
        high_ref[start : start + span, :] = high
        middle_ref[start : start + span, :] = middle
        low_ref[start : start + span, :] = low


def association_kernel(
    sum_hbm, library_ref, high_hbm, middle_hbm, low_hbm, dosage_hbm, windows_ref, out_ref,
    sum_ref, high_ref, middle_ref, low_ref, dosage_ref, sems,
):
    pairs = (
        (sum_hbm, sum_ref),
        (high_hbm, high_ref),
        (middle_hbm, middle_ref),
        (low_hbm, low_ref),
        (dosage_hbm, dosage_ref),
    )
    copies = [
        pltpu.make_async_copy(source, target, sems.at[index])
        for index, (source, target) in enumerate(pairs)
    ]
    for copy in copies:
        copy.start()
    library = library_ref[0]
    for peer in range(1, N):
        library = library + library_ref[peer]
    library = library + 1.0
    copies[0].wait()
    expression = jnp.concatenate(
        [
            jnp.log2((sum_ref[gene * CT : (gene + 1) * CT] + 0.5) / library * 1000000.0)
            for gene in range(OWN)
        ],
        axis=0,
    )
    both = OWN * CT
    parts = jnp.concatenate(split3(expression), axis=0)
    plain = (((1,), (0,)), ((), ()))
    for copy in copies[1:]:
        copy.wait()
    first = lax.dot_general(parts, high_ref[...], plain, preferred_element_type=F32)
    second = lax.dot_general(parts[: 2 * both], middle_ref[...], plain, preferred_element_type=F32)
    third = lax.dot_general(parts[:both], low_ref[...], plain, preferred_element_type=F32)
    residual = (
        (third + second[both:] + first[2 * both :]) + (second[:both] + first[both : 2 * both])
    ) + first[:both]
    upper_part = residual.astype(BF16)
    lower_part = (residual - upper_part.astype(F32)).astype(BF16)
    products = lax.dot_general(
        jnp.concatenate([upper_part, lower_part], axis=0),
        dosage_ref[...],
        NT,
        preferred_element_type=F32,
    )
    products = (products[:both] + products[both:]) * (1.0 / math.sqrt(DONORS))
    windows = windows_ref[...]
    lane = lax.broadcasted_iota(I32, (1, LANES), 1)
    for gene in range(OWN):
        first = jnp.where(lane == 0, windows[gene : gene + 1, :LANES], 0).astype(F32)
        start = jnp.sum(first).astype(I32) & (SNPS - 1)
        turned = pltpu.roll(
            products[gene * CT : (gene + 1) * CT], (SNPS - start) & (SNPS - 1), 1
        )
        live = windows[gene : gene + 1] >= 0
        out_ref[:, gene, :] = jnp.where(live, turned, 0.0)


MIB = 1024 * 1024
HBM = pl.BlockSpec(memory_space=pltpu.HBM)


def whole(dims):
    return pl.BlockSpec(dims, lambda step: (0,) * len(dims))


def call(kernel, name, outs, ins, limit, scratch=()):
    return pl.pallas_call(
        kernel,
        name=name,
        grid=(1,),
        out_shape=outs,
        in_specs=ins,
        out_specs=[whole(out.shape) for out in outs],
        scratch_shapes=scratch,
        compiler_params=pltpu.CompilerParams(vmem_limit_bytes=limit * MIB),
    )


PART_SHAPE = (PEERS, ROWS, LANES)
LIBRARY_SHAPE = (N, CT, DONORS)
SUM_SHAPE = (OWN * CT, DONORS)
SQUARE = (DONORS, DONORS)
DOSAGE_SHAPE = (SNPS, DONORS)

pack = call(
    pack_kernel,
    "pack",
    [jax.ShapeDtypeStruct(PART_SHAPE, F32)],
    [HBM] * 4,
    16,
    [
        pltpu.VMEM((CELLS, GENES), I32),
        pltpu.VMEM((CHUNKS, LANES), I32),
        pltpu.VMEM((CHUNKS, LANES), I32),
        pltpu.VMEM((N, NCOV), F32),
        pltpu.VMEM((N, LANES), F32),
        pltpu.SemaphoreType.DMA((CHUNKS + 3,)),
    ],
)
sum_cells = call(
    sum_kernel,
    "sum_cells",
    [pltpu.HBM(SUM_SHAPE, F32), pltpu.HBM(LIBRARY_SHAPE, F32)],
    [whole(PART_SHAPE)],
    24,
)
project = call(
    projection_kernel,
    "project",
    [pltpu.HBM(SQUARE, BF16)] * 3 + [pltpu.HBM(DOSAGE_SHAPE, BF16)],
    [whole(PART_SHAPE), whole(DOSAGE_SHAPE)],
    32,
)
associate = call(
    association_kernel,
    "associate",
    [jax.ShapeDtypeStruct((CT, OWN, WIN), F32)],
    [HBM, whole(LIBRARY_SHAPE), HBM, HBM, HBM, HBM, whole((OWN, WIN))],
    32,
    [
        pltpu.VMEM(SUM_SHAPE, F32),
        pltpu.VMEM(SQUARE, BF16),
        pltpu.VMEM(SQUARE, BF16),
        pltpu.VMEM(SQUARE, BF16),
        pltpu.VMEM(DOSAGE_SHAPE, BF16),
        pltpu.SemaphoreType.DMA((5,)),
    ],
)


def keep(array):
    return pltpu.with_memory_space_constraint(array, pltpu.HBM)


def per_device(counts, cell_donor, cell_type, covariates, dosage, windows):
    (parts,) = pack(
        keep(counts),
        keep(cell_donor.reshape(CHUNKS, LANES)),
        keep(cell_type.reshape(CHUNKS, LANES)),
        keep(covariates),
    )
    parts = lax.all_to_all(parts, ("cell", "donor"), 0, 0, tiled=True)
    sums, library = sum_cells(parts)
    library = lax.all_to_all(library, "gene", 0, 0, tiled=True)
    high, middle, low, dosage_half = project(parts, dosage)
    return associate(
        keep(sums),
        library,
        keep(high),
        keep(middle),
        keep(low),
        keep(dosage_half),
        windows,
    )[0]


def solution(mesh):
    in_specs = (
        P(("cell", "donor"), "gene"),
        P(("cell", "donor")),
        P(("cell", "donor")),
        P(("cell", "donor"), None),
        P("gene", None),
        P(("gene", "cell", "donor"), None),
    )
    out_specs = P(None, ("gene", "cell", "donor"), None)
    return jax.shard_map(
        per_device, mesh=mesh, in_specs=in_specs, out_specs=out_specs, check_vma=False
    )
```

time: 93.3 us -> 74.8 us (0.80)
  the two profiles are of different devices: /device:TPU:1 before, /device:TPU:2 now
where the time goes in v2:
time: 74.8 us; the launch traced here: 74.4 us
  blocking collectives  42.6 us (57%)
  Pallas kernels  19.1 us (26%)
  starting transfers between devices  7.23 us (10%)
  waiting for transfers between devices  5.48 us (7%)
    all_to_all x1, blocking collectives, per_device(): parts = lax.all_to_all(parts, ('cell', 'donor'), 0, 0, tiled=True)  42.6 us
    pallas_call x1, Pallas kernels, per_device(): high, middle, low, dosage_half = project(parts, dosage)  8.21 us
    all_to_all x1, starting transfers between devices, per_device(): library = lax.all_to_all(library, 'gene', 0, 0, tiled=True)  7.23 us
    pallas_call x1, Pallas kernels, per_device(): sums, library = sum_cells(parts)  5.63 us
    all_to_all x1, waiting for transfers between devices, per_device(): library = lax.all_to_all(library, 'gene', 0, 0, tiled=True)  5.48 us
    pallas_call x1, Pallas kernels, per_device(): associate(keep(sums), library, keep(high), keep(middle), keep(low), keep(...  3.67 us
    pallas_call x1, Pallas kernels, per_device(): pack(keep(counts), keep(cell_donor.reshape(CHUNKS, LANES)), keep(cell_typ...  1.58 us
  transfers between devices with their start and end apart: 1, of which 1 were waited for; matrix products, arithmetic and copies ran while one was open for 0% of the time, Pallas kernels for 11%

profile of v2, /device:TPU:2, one launch (start us, length us, event | category | flops | bytes accessed | tf_op | source)
XLA Modules:
  0.0 74.4 jit_solution(15241436525476421573)
XLA Ops:
  0.0 1.6 %pack.1 = f32[64,32,128]{2,1,0:T(8,128)S(1)} custom-call(s32[512,256]{1,0:T(8,128)} %counts_hbm.1, s32[4,128]{1,0:T(4,128)} %bitcast.2, s32[4,128]{1,0:T(4,128)} %bitcast.3, f32[8,50]{1,0:T(8,128)} %cov_hbm.1), custom_call_target="tpu_custom_call" | custom-call | tf_op jit(solution)/shard_map/pack/pallas_call | solution.py:335
  1.6 0.0 copy-start
  1.6 42.6 %all_to_all.10.part_ref = f32[64,32,128]{2,1,0:T(8,128)S(1)} all-to-all(f32[64,32,128]{2,1,0:T(8,128)S(1)} %pack.1), channel_id=1, replica_groups=mesh['cell'=8,'donor'=8,'gene'=8] {'cell','donor'}, dimensions={0} | all-to-all | bytes 2097152 | tf_op jit(solution)/shard_map/all_to_all | solution.py:341
  44.2 5.6 %sum_cells.1 = (f32[96,512]{1,0:T(8,128)}, f32[8,24,512]{2,1,0:T(8,128)}) custom-call(f32[64,32,128]{2,1,0:T(8,128)S(1)} %all_to_all.10.part_ref), custom_call_target="tpu_custom_call" | custom-call | tf_op jit(solution)/shard_map/sum_cells/pallas_call | solution.py:342
  49.8 0.0 copy-start.1
  49.8 7.2 %all-to-all-start.1 = ((f32[8,24,512]{2,1,0:T(8,128)}), f32[8,24,512]{2,1,0:T(8,128)S(1)}, u32[]{:S(2)}, u32[]{:S(2)}) async-start(f32[8,24,512]{2,1,0:T(8,128)} %get-tuple-element.12), calls=%async_computation.1 | async-start | bytes 786432 | tf_op jit(solution)/shard_map/all_to_all | solution.py:343
  57.1 0.0 copy-done
  57.1 8.2 %project.1 = (bf16[512,512]{1,0:T(8,128)(2,1)}, bf16[512,512]{1,0:T(8,128)(2,1)}, bf16[512,512]{1,0:T(8,128)(2,1)}, bf16[1024,512]{1,0:T(8,128)(2,1)}) custom-call(f32[64,32,128]{2,1,0:T(8,128)S(1)} %all_to_all.10.part_ref, s32[1024,512]{1,0:T(8,128)S(1)} %copy-done), custom_call_target="tpu_custom_call" | custom-call | tf_op jit(solution)/shard_map/project/pallas_call | solution.py:344
  65.3 5.5 %all-to-all-done.1.library_ref = f32[8,24,512]{2,1,0:T(8,128)S(1)} async-done(((f32[8,24,512]{2,1,0:T(8,128)}), f32[8,24,512]{2,1,0:T(8,128)S(1)}, u32[]{:S(2)}, u32[]{:S(2)}) %all-to-all-start.1) | async-done | bytes 393248 | tf_op jit(solution)/shard_map/all_to_all | solution.py:343
  70.8 0.0 copy-done.1
  70.8 3.7 %associate.1 = f32[24,4,1024]{2,1,0:T(4,128)} custom-call(f32[96,512]{1,0:T(8,128)} %get-tuple-element.11.sum_hbm, f32[8,24,512]{2,1,0:T(8,128)S(1)} %all-to-all-done.1.library_ref, bf16[512,512]{1,0:T(8,128)(2,1)} %get-tuple-element.13.high_hbm, bf16[512,512]{1,0:T(8,128)(2,1)} %get-tuple-element.14.middle_hbm, bf16[512,512]{1,0:T(8,128)(2,1)} %get-tuple-element.15.low_hbm, ...), custom_call_target="tpu_custom_call" | custom-call | tf_op jit(solution)/shard_map/associate/pallas_call | solution.py:345
Async XLA Ops:
  1.6 55.5 %copy-start = (s32[1024,512]{1,0:T(8,128)S(1)}, s32[1024,512]{1,0:T(8,128)}, u32[]{:S(2)}) copy-start(s32[1024,512]{1,0:T(8,128)} %dosage_ref.1) | copy-start | bytes 6291460
  49.8 20.9 %copy-start.1 = (s32[4,1024]{1,0:T(4,128)S(1)}, s32[4,1024]{1,0:T(4,128)}, u32[]{:S(2)}) copy-start(s32[4,1024]{1,0:T(4,128)} %windows_ref.1) | copy-start | bytes 49156
  49.8 20.9 %all-to-all-start.1 = ((f32[8,24,512]{2,1,0:T(8,128)}), f32[8,24,512]{2,1,0:T(8,128)S(1)}, u32[]{:S(2)}, u32[]{:S(2)}) async-start(f32[8,24,512]{2,1,0:T(8,128)} %get-tuple-element.12), calls=%async_computation.1 | async-start | bytes 786432 | tf_op jit(solution)/shard_map/all_to_all | solution.py:343

commit v3 on v2

--- a/solution.py
+++ b/solution.py
@@ -89,39 +89,43 @@
     return jnp.concatenate([block[row : row + 1] for row in range(CHUNKS)], axis=1)
 
 
-def sum_kernel(part_ref, sum_ref, library_ref):
+def sum_kernel(part_ref, sum_hbm, library_hbm, sum_ref, library_ref, sems):
     lane = lax.broadcasted_iota(I32, (KINDS * SUB, LANES), 1)
+    place = lax.broadcasted_iota(I32, (PARTS * DON_GRP, CELLS), 0)
+    place = place.astype(F32).astype(BF16)
+    step = lax.broadcasted_iota(I32, (SUB, CELLS), 0)
 
     def one_block(block):
-        block_rows = part_ref[block]
-        donor = to_row(block_rows[DONOR_ROW:TYPE_ROW]).astype(I32)
-        kind = to_row(block_rows[TYPE_ROW:TOTAL_ROW]).astype(I32)
+        donor = part_ref[block, DONOR_ROW:TYPE_ROW, :].astype(I32)
+        kind = part_ref[block, TYPE_ROW:TOTAL_ROW, :].astype(I32)
         local = ((donor >> 6) << 3) + (donor & 7)
         column = jnp.where(kind >= 0, ((kind >> 3) << 6) + local, -1)
-        place = lax.broadcasted_iota(I32, (PARTS * DON_GRP, CELLS), 0)
-        onehot = jnp.where(place == column, 1.0, 0.0).astype(BF16)
-        wanted = lax.broadcasted_iota(I32, (SUB, CELLS), 0) == (kind & 7)
-        total = to_row(block_rows[TOTAL_ROW:COV_ROW])
+        column = to_row(column.astype(F32)).astype(BF16)
+        one, zero = jnp.ones((), BF16), jnp.zeros((), BF16)
+        onehot = jnp.where(place == column, one, zero)
+        wanted = step == to_row(kind & 7)
+        total = part_ref[block, TOTAL_ROW:COV_ROW, :]
         high = total.astype(BF16).astype(F32)
         values = [
             jnp.concatenate(
                 [
-                    block_rows[chunk * OWN + gene : chunk * OWN + gene + 1]
+                    part_ref[block, chunk * OWN + gene : chunk * OWN + gene + 1, :]
                     for chunk in range(CHUNKS)
                 ],
                 axis=1,
             )
             for gene in range(OWN)
         ]
-        values += [high, total - high]
+        values += [to_row(high), to_row(total - high)]
         left = jnp.concatenate([jnp.where(wanted, value, 0.0) for value in values], axis=0)
-        return lax.dot_general(left.astype(BF16), onehot, NT, preferred_element_type=F32)
+        return lax.dot_general(onehot, left.astype(BF16), NT, preferred_element_type=F32)
 
     def one_pair(pair, carry):
         even, odd = one_block(2 * pair), one_block(2 * pair + 1)
         for cell in range(1, N):
             even = even + one_block(cell * N + 2 * pair)
             odd = odd + one_block(cell * N + 2 * pair + 1)
+        even, odd = even.T, odd.T
         even_low, odd_low = even[:, :LANES], odd[:, :LANES]
         merged = [
             jnp.where(lane < DON_GRP, even_low, pltpu.roll(odd_low, DON_GRP, 1)),
@@ -134,15 +138,28 @@
                 start = gene * CT + part * SUB
                 sum_ref[start : start + SUB, span] = value[gene * SUB : (gene + 1) * SUB]
             library = value[OWN * SUB : (OWN + 1) * SUB] + value[(OWN + 1) * SUB :]
-            for peer in range(N):
-                library_ref[peer, part * SUB : (part + 1) * SUB, span] = library
+            library_ref[part * SUB : (part + 1) * SUB, span] = library
         return carry
 
     lax.fori_loop(0, N // 2, one_pair, 0)
-
-
-def projection_kernel(part_ref, dosage_ref, high_ref, middle_ref, low_ref, dosage_out_ref):
-    dosage_out_ref[...] = dosage_ref[...].astype(F32).astype(BF16)
+    copies = [
+        pltpu.make_async_copy(library_ref, library_hbm.at[peer], sems.at[peer])
+        for peer in range(N)
+    ]
+    copies.append(pltpu.make_async_copy(sum_ref, sum_hbm, sems.at[N]))
+    for copy in copies:
+        copy.start()
+    for copy in copies:
+        copy.wait()
+
+
+def projection_kernel(
+    part_ref, dosage_ref, high_hbm, middle_hbm, low_hbm, dosage_hbm,
+    high_ref, middle_ref, low_ref, half_ref, sems,
+):
+    half_ref[...] = dosage_ref[...].astype(F32).astype(BF16)
+    copies = [pltpu.make_async_copy(half_ref, dosage_hbm, sems.at[0])]
+    copies[0].start()
     lane = lax.broadcasted_iota(I32, (SUB, LANES), 1)
     first_half = lax.broadcasted_iota(I32, (SUB, LANES), 0) < N // 2
     tiles = []
@@ -161,11 +178,18 @@
     lane_id = lax.broadcasted_iota(I32, (rows, LANES), 1)
     work = jnp.where(lane_id < 64, gram[:rows], jnp.where(lane_id - 64 == row_id, 1.0, 0.0))
     row_col = lax.broadcasted_iota(I32, (rows, 1), 0)
-    for column in range(ORDER):
-        pivot_row = work[column : column + 1, :]
-        scaled = pivot_row / pivot_row[:, column : column + 1]
-        below = jnp.where(row_col > column, work[:, column : column + 1], 0.0)
-        work = work - below * scaled
+    for panel in range(0, ORDER, SUB):
+        members = range(panel, min(panel + SUB, ORDER))
+        held = {
+            column: jnp.broadcast_to(work[:, column : column + 1], (rows, LANES))
+            for column in members
+        }
+        for column in members:
+            mine = held[column]
+            factor = jnp.where(row_id > column, mine, 0.0) * (1.0 / mine[column : column + 1])
+            for later in range(column + 1, members.stop):
+                held[later] = held[later] - factor * mine[later : later + 1]
+            work = work - factor * work[column : column + 1]
     pivots = jnp.sum(jnp.where(lane_id == row_id, work, 0.0), axis=1, keepdims=True)
     scale = 1.0 / jnp.sqrt(jnp.where(row_col < ORDER, pivots, 1.0))
     inverse = pltpu.roll(work, 64, 1)
@@ -175,9 +199,9 @@
         inverse, turned, (((1,), (0,)), ((), ())), precision=HIGHEST, preferred_element_type=F32
     )
     span = 128
+    column = lax.broadcasted_iota(I32, (span, DONORS), 1)
     for start in range(0, DONORS, span):
-        row = lax.broadcasted_iota(I32, (span, DONORS), 0) + start
-        column = lax.broadcasted_iota(I32, (span, DONORS), 1)
+        row = lax.broadcasted_iota(I32, (span, 1), 0) + start
         same = (((row >> 3) & 7) << 6) + ((row >> 6) << 3) + (row & 7) == column
         fitted = lax.dot_general(
             left[start : start + span],
@@ -187,10 +211,17 @@
             preferred_element_type=F32,
         )
         kept = jnp.where(same, 1.0, 0.0) - fitted
-        high, middle, low = split3(kept)
-        high_ref[start : start + span, :] = high
-        middle_ref[start : start + span, :] = middle
-        low_ref[start : start + span, :] = low
+        targets = ((high_ref, high_hbm), (middle_ref, middle_hbm), (low_ref, low_hbm))
+        for (held_ref, target), piece in zip(targets, split3(kept)):
+            held_ref[start : start + span, :] = piece
+            rows_here = pl.ds(start, span)
+            copy = pltpu.make_async_copy(
+                held_ref.at[rows_here], target.at[rows_here], sems.at[len(copies)]
+            )
+            copy.start()
+            copies.append(copy)
+    for copy in copies:
+        copy.wait()
 
 
 def association_kernel(
@@ -225,16 +256,18 @@
     both = OWN * CT
     parts = jnp.concatenate(split3(expression), axis=0)
     plain = (((1,), (0,)), ((), ()))
-    for copy in copies[1:]:
-        copy.wait()
+    copies[1].wait()
     first = lax.dot_general(parts, high_ref[...], plain, preferred_element_type=F32)
+    copies[2].wait()
     second = lax.dot_general(parts[: 2 * both], middle_ref[...], plain, preferred_element_type=F32)
+    copies[3].wait()
     third = lax.dot_general(parts[:both], low_ref[...], plain, preferred_element_type=F32)
     residual = (
         (third + second[both:] + first[2 * both :]) + (second[:both] + first[both : 2 * both])
     ) + first[:both]
     upper_part = residual.astype(BF16)
     lower_part = (residual - upper_part.astype(F32)).astype(BF16)
+    copies[4].wait()
     products = lax.dot_general(
         jnp.concatenate([upper_part, lower_part], axis=0),
         dosage_ref[...],
@@ -258,18 +291,16 @@
 HBM = pl.BlockSpec(memory_space=pltpu.HBM)
 
 
-def whole(dims):
-    return pl.BlockSpec(dims, lambda step: (0,) * len(dims))
+VMEM = pl.BlockSpec(memory_space=pltpu.VMEM)
 
 
 def call(kernel, name, outs, ins, limit, scratch=()):
     return pl.pallas_call(
         kernel,
         name=name,
-        grid=(1,),
-        out_shape=outs,
+        out_shape=[out for out, _ in outs],
         in_specs=ins,
-        out_specs=[whole(out.shape) for out in outs],
+        out_specs=[spec for _, spec in outs],
         scratch_shapes=scratch,
         compiler_params=pltpu.CompilerParams(vmem_limit_bytes=limit * MIB),
     )
@@ -284,9 +315,9 @@
 pack = call(
     pack_kernel,
     "pack",
-    [jax.ShapeDtypeStruct(PART_SHAPE, F32)],
+    [(jax.ShapeDtypeStruct(PART_SHAPE, F32), VMEM)],
     [HBM] * 4,
-    16,
+    8,
     [
         pltpu.VMEM((CELLS, GENES), I32),
         pltpu.VMEM((CHUNKS, LANES), I32),
@@ -299,31 +330,33 @@
 sum_cells = call(
     sum_kernel,
     "sum_cells",
-    [pltpu.HBM(SUM_SHAPE, F32), pltpu.HBM(LIBRARY_SHAPE, F32)],
-    [whole(PART_SHAPE)],
-    24,
+    [(pltpu.HBM(SUM_SHAPE, F32), HBM), (pltpu.HBM(LIBRARY_SHAPE, F32), HBM)],
+    [VMEM],
+    16,
+    [
+        pltpu.VMEM(SUM_SHAPE, F32),
+        pltpu.VMEM((CT, DONORS), F32),
+        pltpu.SemaphoreType.DMA((N + 1,)),
+    ],
 )
+MATRICES = (SQUARE, SQUARE, SQUARE, DOSAGE_SHAPE)
 project = call(
     projection_kernel,
     "project",
-    [pltpu.HBM(SQUARE, BF16)] * 3 + [pltpu.HBM(DOSAGE_SHAPE, BF16)],
-    [whole(PART_SHAPE), whole(DOSAGE_SHAPE)],
-    32,
+    [(pltpu.HBM(dims, BF16), HBM) for dims in MATRICES],
+    [VMEM, VMEM],
+    16,
+    [pltpu.VMEM(dims, BF16) for dims in MATRICES] + [pltpu.SemaphoreType.DMA((13,))],
 )
 associate = call(
     association_kernel,
     "associate",
-    [jax.ShapeDtypeStruct((CT, OWN, WIN), F32)],
-    [HBM, whole(LIBRARY_SHAPE), HBM, HBM, HBM, HBM, whole((OWN, WIN))],
-    32,
-    [
-        pltpu.VMEM(SUM_SHAPE, F32),
-        pltpu.VMEM(SQUARE, BF16),
-        pltpu.VMEM(SQUARE, BF16),
-        pltpu.VMEM(SQUARE, BF16),
-        pltpu.VMEM(DOSAGE_SHAPE, BF16),
-        pltpu.SemaphoreType.DMA((5,)),
-    ],
+    [(jax.ShapeDtypeStruct((CT, OWN, WIN), F32), VMEM)],
+    [HBM, VMEM, HBM, HBM, HBM, HBM, VMEM],
+    16,
+    [pltpu.VMEM(SUM_SHAPE, F32)]
+    + [pltpu.VMEM(dims, BF16) for dims in MATRICES]
+    + [pltpu.SemaphoreType.DMA((5,))],
 )
 
 

time: 74.8 us -> 73.9 us (0.988)
  Pallas kernels: 19.1 us -> 15.2 us
  waiting for transfers between devices: 5.48 us -> 8.64 us
    pallas_call x1, Pallas kernels: 8.21 us -> 5.04 us  [per_device(): high, middle, low, dosage_half = project(parts, dosage)]
    all_to_all x1, waiting for transfers between devices: 5.48 us -> 8.64 us  [per_device(): library = lax.all_to_all(library, 'gene', 0, 0, tiled=True)]
  transfers between devices with their start and end apart: 1 -> 1, of which waited for: 1 -> 1; matrix products, arithmetic and copies ran while one was open for 0% -> 0% of each run, Pallas kernels for 11% -> 7%
where the time goes in v3:
time: 73.9 us; the launch traced here: 73.6 us
  blocking collectives  42.6 us (58%)
  Pallas kernels  15.2 us (21%)
  waiting for transfers between devices  8.64 us (12%)
  starting transfers between devices  7.11 us (10%)
    all_to_all x1, blocking collectives, per_device(): parts = lax.all_to_all(parts, ('cell', 'donor'), 0, 0, tiled=True)  42.6 us
    all_to_all x1, waiting for transfers between devices, per_device(): library = lax.all_to_all(library, 'gene', 0, 0, tiled=True)  8.64 us
    all_to_all x1, starting transfers between devices, per_device(): library = lax.all_to_all(library, 'gene', 0, 0, tiled=True)  7.11 us
    pallas_call x1, Pallas kernels, per_device(): sums, library = sum_cells(parts)  5.28 us
    pallas_call x1, Pallas kernels, per_device(): high, middle, low, dosage_half = project(parts, dosage)  5.04 us
    pallas_call x1, Pallas kernels, per_device(): associate(keep(sums), library, keep(high), keep(middle), keep(low), keep(...  3.28 us
    pallas_call x1, Pallas kernels, per_device(): pack(keep(counts), keep(cell_donor.reshape(CHUNKS, LANES)), keep(cell_typ...  1.58 us
  transfers between devices with their start and end apart: 1, of which 1 were waited for; matrix products, arithmetic and copies ran while one was open for 0% of the time, Pallas kernels for 7%

profile of v3, /device:TPU:2, one launch (start us, length us, event | category | flops | bytes accessed | tf_op | source)
XLA Modules:
  0.0 73.6 jit_solution(2614845830619506524)
XLA Ops:
  0.0 1.6 %pack.1 = f32[64,32,128]{2,1,0:T(8,128)S(1)} custom-call(s32[512,256]{1,0:T(8,128)} %counts_hbm.1, s32[4,128]{1,0:T(4,128)} %bitcast.2, s32[4,128]{1,0:T(4,128)} %bitcast.3, f32[8,50]{1,0:T(8,128)} %cov_hbm.1), custom_call_target="tpu_custom_call" | custom-call | tf_op jit(solution)/shard_map/pack/pallas_call | solution.py:368
  1.6 0.0 copy-start
  1.6 42.6 %all_to_all.10.part_ref = f32[64,32,128]{2,1,0:T(8,128)S(1)} all-to-all(f32[64,32,128]{2,1,0:T(8,128)S(1)} %pack.1), channel_id=1, replica_groups=mesh['cell'=8,'donor'=8,'gene'=8] {'cell','donor'}, dimensions={0} | all-to-all | bytes 2097152 | tf_op jit(solution)/shard_map/all_to_all | solution.py:374
  44.2 5.3 %sum_cells.1 = (f32[96,512]{1,0:T(8,128)}, f32[8,24,512]{2,1,0:T(8,128)}) custom-call(f32[64,32,128]{2,1,0:T(8,128)S(1)} %all_to_all.10.part_ref), custom_call_target="tpu_custom_call" | custom-call | tf_op jit(solution)/shard_map/sum_cells/pallas_call | solution.py:375
  49.5 0.0 copy-start.1
  49.5 7.1 %all-to-all-start.1 = ((f32[8,24,512]{2,1,0:T(8,128)}), f32[8,24,512]{2,1,0:T(8,128)S(1)}, u32[]{:S(2)}, u32[]{:S(2)}) async-start(f32[8,24,512]{2,1,0:T(8,128)} %get-tuple-element.12), calls=%async_computation.1 | async-start | bytes 786432 | tf_op jit(solution)/shard_map/all_to_all | solution.py:376
  56.6 0.0 copy-done
  56.6 5.0 %project.1 = (bf16[512,512]{1,0:T(8,128)(2,1)}, bf16[512,512]{1,0:T(8,128)(2,1)}, bf16[512,512]{1,0:T(8,128)(2,1)}, bf16[1024,512]{1,0:T(8,128)(2,1)}) custom-call(f32[64,32,128]{2,1,0:T(8,128)S(1)} %all_to_all.10.part_ref, s32[1024,512]{1,0:T(8,128)S(1)} %copy-done), custom_call_target="tpu_custom_call" | custom-call | tf_op jit(solution)/shard_map/project/pallas_call | solution.py:377
  61.7 8.6 %all-to-all-done.1.library_ref = f32[8,24,512]{2,1,0:T(8,128)S(1)} async-done(((f32[8,24,512]{2,1,0:T(8,128)}), f32[8,24,512]{2,1,0:T(8,128)S(1)}, u32[]{:S(2)}, u32[]{:S(2)}) %all-to-all-start.1) | async-done | bytes 393248 | tf_op jit(solution)/shard_map/all_to_all | solution.py:376
  70.3 0.0 copy-done.1
  70.3 3.3 %associate.1 = f32[24,4,1024]{2,1,0:T(4,128)} custom-call(f32[96,512]{1,0:T(8,128)} %get-tuple-element.11.sum_hbm, f32[8,24,512]{2,1,0:T(8,128)S(1)} %all-to-all-done.1.library_ref, bf16[512,512]{1,0:T(8,128)(2,1)} %get-tuple-element.13.high_hbm, bf16[512,512]{1,0:T(8,128)(2,1)} %get-tuple-element.14.middle_hbm, bf16[512,512]{1,0:T(8,128)(2,1)} %get-tuple-element.15.low_hbm, ...), custom_call_target="tpu_custom_call" | custom-call | tf_op jit(solution)/shard_map/associate/pallas_call | solution.py:378
Async XLA Ops:
  1.6 55.0 %copy-start = (s32[1024,512]{1,0:T(8,128)S(1)}, s32[1024,512]{1,0:T(8,128)}, u32[]{:S(2)}) copy-start(s32[1024,512]{1,0:T(8,128)} %dosage_ref.1) | copy-start | bytes 6291460
  49.5 20.8 %copy-start.1 = (s32[4,1024]{1,0:T(4,128)S(1)}, s32[4,1024]{1,0:T(4,128)}, u32[]{:S(2)}) copy-start(s32[4,1024]{1,0:T(4,128)} %windows_ref.1) | copy-start | bytes 49156
  49.5 20.8 %all-to-all-start.1 = ((f32[8,24,512]{2,1,0:T(8,128)}), f32[8,24,512]{2,1,0:T(8,128)S(1)}, u32[]{:S(2)}, u32[]{:S(2)}) async-start(f32[8,24,512]{2,1,0:T(8,128)} %get-tuple-element.12), calls=%async_computation.1 | async-start | bytes 786432 | tf_op jit(solution)/shard_map/all_to_all | solution.py:376

commit v4 on v3

v4 whole, which is shorter than its diff:
```python
import math

import jax
import jax.numpy as jnp
from jax import lax
from jax.experimental import pallas as pl
from jax.experimental.pallas import tpu as pltpu
from jax.sharding import PartitionSpec as P

F32 = jnp.float32
BF16 = jnp.bfloat16
I32 = jnp.int32
HIGHEST = lax.Precision.HIGHEST

CT = 24
HALF = CT // 2
SUB = 8
NCOV = 50
ORDER = NCOV + 1
ORDER_ROWS = 56
N = 8
CELLS = 512
LANES = 128
CHUNKS = CELLS // LANES
GENES = 256
GENE_PART = GENES // N
OWN = GENE_PART // N
DON_GRP = 64
DONORS = N * DON_GRP
SNPS = 1024
WIN = 1024
DONOR_ROW = CHUNKS * GENE_PART
TYPE_ROW = DONOR_ROW + CHUNKS
TOTAL_ROW = TYPE_ROW + CHUNKS
COV_ROW = TOTAL_ROW + CHUNKS
PART_ROWS = COV_ROW + N // 2
SUM_ROWS = HALF * GENE_PART
LIB_ROWS = 16
EXPR_ROWS = HALF * OWN
SEND_ROWS = EXPR_ROWS + N * N // 2

NT = (((1,), (1,)), ((), ()))
PLAIN = (((1,), (0,)), ((), ()))


def pack_kernel(
    counts_hbm, donor_hbm, type_hbm, cov_hbm, part_ref,
    counts_ref, donor_ref, type_ref, cov_ref, wide_ref, sems,
):
    copies = [
        pltpu.make_async_copy(
            counts_hbm.at[pl.ds(chunk * LANES, LANES)],
            counts_ref.at[pl.ds(chunk * LANES, LANES)],
            sems.at[chunk],
        )
        for chunk in range(CHUNKS)
    ]
    copies.append(pltpu.make_async_copy(donor_hbm, donor_ref, sems.at[CHUNKS]))
    copies.append(pltpu.make_async_copy(type_hbm, type_ref, sems.at[CHUNKS + 1]))
    copies.append(pltpu.make_async_copy(cov_hbm, cov_ref, sems.at[CHUNKS + 2]))
    for copy in copies:
        copy.start()
    totals = []
    for chunk in range(CHUNKS):
        copies[chunk].wait()
        turned = counts_ref[chunk * LANES : (chunk + 1) * LANES, :].astype(F32).T
        totals.append(jnp.sum(turned, axis=0, keepdims=True))
        for peer in range(N):
            part_ref[peer, chunk * GENE_PART : (chunk + 1) * GENE_PART, :] = turned[
                peer * GENE_PART : (peer + 1) * GENE_PART
            ]
    for copy in copies[CHUNKS:]:
        copy.wait()
    wide_ref[...] = jnp.zeros_like(wide_ref)
    wide_ref[:, :NCOV] = cov_ref[...]
    wide = wide_ref[...]
    paired = wide[: N // 2] + pltpu.roll(wide, DON_GRP, 1)[N // 2 :]
    shared = jnp.concatenate(
        [donor_ref[...].astype(F32), type_ref[...].astype(F32), *totals, paired], axis=0
    )
    for peer in range(N):
        part_ref[peer, DONOR_ROW:PART_ROWS, :] = shared


def to_row(block):
    return jnp.concatenate([block[row : row + 1] for row in range(CHUNKS)], axis=1)


def read_labels(part_ref, block):
    donor = part_ref[block, DONOR_ROW:TYPE_ROW, :].astype(I32)
    kind = part_ref[block, TYPE_ROW:TOTAL_ROW, :].astype(I32)
    local = ((donor >> 6) << 3) + (donor & 7)
    upper = kind >= HALF
    column = jnp.where(kind >= 0, jnp.where(upper, local + DON_GRP, local), -1)
    place = lax.broadcasted_iota(I32, (LANES, CELLS), 0)
    onehot = jnp.where(place == to_row(column), 1.0, 0.0).astype(BF16)
    return onehot, to_row(jnp.where(upper, kind - HALF, kind))


def library_kernel(part_ref, library_hbm, library_ref, sems):
    number = lax.broadcasted_iota(I32, (LIB_ROWS, CELLS), 0)
    summed = jnp.zeros((2 * LIB_ROWS, LANES), F32)
    for block in range(N):
        onehot, step = read_labels(part_ref, block)
        total = part_ref[block, TOTAL_ROW:COV_ROW, :]
        high = total.astype(BF16).astype(F32)
        left = jnp.concatenate(
            [jnp.where(number == step, to_row(value), 0.0) for value in (high, total - high)],
            axis=0,
        )
        summed = summed + lax.dot_general(
            left.astype(BF16), onehot, NT, preferred_element_type=F32
        )
    library_ref[...] = summed[:LIB_ROWS] + summed[LIB_ROWS:]
    copies = [
        pltpu.make_async_copy(library_ref, library_hbm.at[peer], sems.at[peer])
        for peer in range(N)
    ]
    for copy in copies:
        copy.start()
    for copy in copies:
        copy.wait()


def sum_kernel(part_ref, sum_hbm, sum_ref, sem):
    sum_ref[...] = jnp.zeros_like(sum_ref)

    def one_block(block, carry):
        onehot, step = read_labels(part_ref, block)
        counts = jnp.concatenate(
            [
                part_ref[block, chunk * GENE_PART : (chunk + 1) * GENE_PART, :]
                for chunk in range(CHUNKS)
            ],
            axis=1,
        )
        step = jnp.broadcast_to(step, (GENE_PART, CELLS))
        left = jnp.concatenate(
            [jnp.where(step == number, counts, 0.0).astype(BF16) for number in range(HALF)],
            axis=0,
        )
        sum_ref[...] += lax.dot_general(left, onehot, NT, preferred_element_type=F32)
        return carry

    lax.fori_loop(0, N, one_block, 0)
    copy = pltpu.make_async_copy(sum_ref, sum_hbm, sem)
    copy.start()
    copy.wait()


def expression_kernel(part_ref, sum_hbm, library_ref, out_ref, sum_ref, sem):
    copy = pltpu.make_async_copy(sum_hbm, sum_ref, sem)
    copy.start()
    for cell in range(N):
        row = EXPR_ROWS + cell * (N // 2)
        packed = part_ref[cell, COV_ROW:PART_ROWS, :]
        for peer in range(N):
            out_ref[peer, row : row + N // 2, :] = packed
    library = library_ref[0]
    for peer in range(1, N):
        library = library + library_ref[peer]
    library = library + 1.0
    copy.wait()
    for step in range(HALF):
        summed = sum_ref[step * GENE_PART : (step + 1) * GENE_PART, :]
        expression = jnp.log2((summed + 0.5) / library[step : step + 1] * 1000000.0)
        for peer in range(N):
            out_ref[peer, step * OWN : (step + 1) * OWN, :] = expression[
                peer * OWN : (peer + 1) * OWN
            ]


def dosage_kernel(dosage_ref, out_hbm, out_ref, sem):
    row = lax.broadcasted_iota(I32, (DONORS, DONORS), 0)
    place = lax.broadcasted_iota(I32, (1, DONORS), 1)
    source = (((place >> 3) & 7) << 6) + ((place >> 6) << 3) + (place & 7)
    order = jnp.where(row == source, 1.0, 0.0).astype(BF16)
    span = 256
    for start in range(0, SNPS, span):
        half = dosage_ref[start : start + span, :].astype(F32).astype(BF16)
        moved = lax.dot_general(half, order, PLAIN, preferred_element_type=F32)
        out_ref[start : start + span, :] = moved.astype(BF16)
    copy = pltpu.make_async_copy(out_ref, out_hbm, sem)
    copy.start()
    copy.wait()


def association_kernel(
    recv_ref, dosage_hbm, windows_ref, out_ref, dosage_ref, expression_ref, sem
):
    copy = pltpu.make_async_copy(dosage_hbm, dosage_ref, sem)
    copy.start()
    lane = lax.broadcasted_iota(I32, (SUB, LANES), 1)
    first_half = lax.broadcasted_iota(I32, (SUB, LANES), 0) < N // 2
    tiles = []
    for donor in range(N):
        for pair in range(N // 2):
            row = EXPR_ROWS + pair * SUB
            tile = recv_ref[donor, row : row + SUB, :]
            other = pltpu.roll(tile, DON_GRP, 1)
            tiles.append(jnp.where(first_half, tile, pltpu.roll(other, N // 2, 0)))
            tiles.append(jnp.where(first_half, pltpu.roll(tile, N // 2, 0), other))
    ends = jnp.where(lane == NCOV, 1.0, 0.0)
    design = jnp.concatenate([jnp.where(lane < NCOV, tile, ends) for tile in tiles], axis=0)
    turned = design.T
    gram = lax.dot_general(turned, turned, NT, precision=HIGHEST, preferred_element_type=F32)
    rows = ORDER_ROWS
    row_id = lax.broadcasted_iota(I32, (rows, LANES), 0)
    lane_id = lax.broadcasted_iota(I32, (rows, LANES), 1)
    row_col = lax.broadcasted_iota(I32, (rows, 1), 0)
    work = jnp.where(lane_id < 64, gram[:rows], jnp.where(lane_id - 64 == row_id, 1.0, 0.0))
    for panel in range(0, ORDER, SUB):
        members = range(panel, min(panel + SUB, ORDER))
        held = {
            column: jnp.broadcast_to(work[:, column : column + 1], (rows, LANES))
            for column in members
        }
        for column in members:
            mine = held[column]
            factor = jnp.where(row_id > column, mine, 0.0) * (1.0 / mine[column : column + 1])
            for later in range(column + 1, members.stop):
                held[later] = held[later] - factor * mine[later : later + 1]
            work = work - factor * work[column : column + 1]
    pivots = jnp.sum(jnp.where(lane_id == row_id, work, 0.0), axis=1, keepdims=True)
    scale = 1.0 / jnp.sqrt(jnp.where(row_col < ORDER, pivots, 1.0))
    inverse = pltpu.roll(work, 64, 1)
    inverse = jnp.where((lane_id < ORDER) & (row_id < ORDER), inverse * scale, 0.0)
    basis = lax.dot_general(inverse, turned, PLAIN, precision=HIGHEST, preferred_element_type=F32)
    wide_lane = lax.broadcasted_iota(I32, (EXPR_ROWS, LANES), 1)
    for pair in range(N // 2):
        one, two = recv_ref[2 * pair, :EXPR_ROWS, :], recv_ref[2 * pair + 1, :EXPR_ROWS, :]
        expression_ref[pair, :EXPR_ROWS, :] = jnp.where(
            wide_lane < DON_GRP, one, pltpu.roll(two, DON_GRP, 1)
        )
        expression_ref[pair, EXPR_ROWS:, :] = jnp.where(
            wide_lane < DON_GRP, pltpu.roll(one, DON_GRP, 1), two
        )
    expression = jnp.concatenate(
        [
            jnp.concatenate(
                [
                    expression_ref[pair, pl.ds(gene, CT, stride=OWN), :]
                    for gene in range(OWN)
                ],
                axis=0,
            )
            for pair in range(N // 2)
        ],
        axis=1,
    )
    fit = lax.dot_general(expression, basis, NT, precision=HIGHEST, preferred_element_type=F32)
    residual = expression - lax.dot_general(
        fit, basis, PLAIN, precision=HIGHEST, preferred_element_type=F32
    )
    upper_part = residual.astype(BF16)
    lower_part = (residual - upper_part.astype(F32)).astype(BF16)
    copy.wait()
    products = lax.dot_general(
        jnp.concatenate([upper_part, lower_part], axis=0),
        dosage_ref[...],
        NT,
        preferred_element_type=F32,
    )
    both = OWN * CT
    products = (products[:both] + products[both:]) * (1.0 / math.sqrt(DONORS))
    windows = windows_ref[...]
    first_lane = lax.broadcasted_iota(I32, (1, LANES), 1) == 0
    for gene in range(OWN):
        first = jnp.where(first_lane, windows[gene : gene + 1, :LANES], 0).astype(F32)
        start = jnp.sum(first).astype(I32) & (SNPS - 1)
        turned_back = pltpu.roll(
            products[gene * CT : (gene + 1) * CT], (SNPS - start) & (SNPS - 1), 1
        )
        live = windows[gene : gene + 1] >= 0
        out_ref[:, gene, :] = jnp.where(live, turned_back, 0.0)


MIB = 1024 * 1024
HBM = pl.BlockSpec(memory_space=pltpu.HBM)


VMEM = pl.BlockSpec(memory_space=pltpu.VMEM)


def call(kernel, name, outs, ins, limit, scratch=()):
    return pl.pallas_call(
        kernel,
        name=name,
        out_shape=[out for out, _ in outs],
        in_specs=ins,
        out_specs=[spec for _, spec in outs],
        scratch_shapes=scratch,
        compiler_params=pltpu.CompilerParams(vmem_limit_bytes=limit * MIB),
    )


PART_SHAPE = (N, PART_ROWS, LANES)
SUM_SHAPE = (SUM_ROWS, LANES)
LIBRARY_SHAPE = (N, LIB_ROWS, LANES)
SEND_SHAPE = (N, SEND_ROWS, LANES)
DOSAGE_SHAPE = (SNPS, DONORS)
DMA = pltpu.SemaphoreType.DMA

pack = call(
    pack_kernel,
    "pack",
    [(jax.ShapeDtypeStruct(PART_SHAPE, F32), VMEM)],
    [HBM] * 4,
    8,
    [
        pltpu.VMEM((CELLS, GENES), I32),
        pltpu.VMEM((CHUNKS, LANES), I32),
        pltpu.VMEM((CHUNKS, LANES), I32),
        pltpu.VMEM((N, NCOV), F32),
        pltpu.VMEM((N, LANES), F32),
        DMA((CHUNKS + 3,)),
    ],
)
sum_library = call(
    library_kernel,
    "sum_library",
    [(pltpu.HBM(LIBRARY_SHAPE, F32), HBM)],
    [VMEM],
    8,
    [pltpu.VMEM(LIBRARY_SHAPE[1:], F32), DMA((N,))],
)
sum_cells = call(
    sum_kernel,
    "sum_cells",
    [(pltpu.HBM(SUM_SHAPE, F32), HBM)],
    [VMEM],
    16,
    [pltpu.VMEM(SUM_SHAPE, F32), DMA],
)
express = call(
    expression_kernel,
    "express",
    [(jax.ShapeDtypeStruct(SEND_SHAPE, F32), VMEM)],
    [VMEM, HBM, VMEM],
    8,
    [pltpu.VMEM(SUM_SHAPE, F32), DMA],
)
order_dosage = call(
    dosage_kernel,
    "order_dosage",
    [(pltpu.HBM(DOSAGE_SHAPE, BF16), HBM)],
    [VMEM],
    16,
    [pltpu.VMEM(DOSAGE_SHAPE, BF16), DMA],
)
associate = call(
    association_kernel,
    "associate",
    [(jax.ShapeDtypeStruct((CT, OWN, WIN), F32), VMEM)],
    [VMEM, HBM, VMEM],
    16,
    [pltpu.VMEM(DOSAGE_SHAPE, BF16), pltpu.VMEM((N // 2, OWN * CT, LANES), F32), DMA],
)


def keep(array):
    return pltpu.with_memory_space_constraint(array, pltpu.HBM)


def per_device(counts, cell_donor, cell_type, covariates, dosage, windows):
    (parts,) = pack(
        keep(counts),
        keep(cell_donor.reshape(CHUNKS, LANES)),
        keep(cell_type.reshape(CHUNKS, LANES)),
        keep(covariates),
    )
    parts = lax.all_to_all(parts, "cell", 0, 0, tiled=True)
    (ordered,) = order_dosage(dosage)
    (library,) = sum_library(parts)
    library = lax.all_to_all(library, "gene", 0, 0, tiled=True)
    (sums,) = sum_cells(parts)
    (sent,) = express(parts, keep(sums), library)
    sent = lax.all_to_all(sent, "donor", 0, 0, tiled=True)
    return associate(sent, keep(ordered), windows)[0]


def solution(mesh):
    in_specs = (
        P(("cell", "donor"), "gene"),
        P(("cell", "donor")),
        P(("cell", "donor")),
        P(("cell", "donor"), None),
        P("gene", None),
        P(("gene", "cell", "donor"), None),
    )
    out_specs = P(None, ("gene", "cell", "donor"), None)
    return jax.shard_map(
        per_device, mesh=mesh, in_specs=in_specs, out_specs=out_specs, check_vma=False
    )
```

time: 73.9 us -> 67.6 us (0.915)
  the two profiles are of different devices: /device:TPU:2 before, /device:TPU:1 now
where the time goes in v4:
time: 67.6 us; the launch traced here: 67.1 us
  blocking collectives  28.2 us (42%)
  starting transfers between devices  14.9 us (22%)
  Pallas kernels  14.1 us (21%)
  waiting for transfers between devices  9.8 us (14%)
    all_to_all x1, blocking collectives, per_device(): parts = lax.all_to_all(parts, 'cell', 0, 0, tiled=True)  28.2 us
    all_to_all x1, starting transfers between devices, per_device(): sent = lax.all_to_all(sent, 'donor', 0, 0, tiled=True)  8.05 us
    all_to_all x1, starting transfers between devices, per_device(): library = lax.all_to_all(library, 'gene', 0, 0, tiled=True)  6.83 us
    all_to_all x1, waiting for transfers between devices, per_device(): sent = lax.all_to_all(sent, 'donor', 0, 0, tiled=True)  5.39 us
    pallas_call x1, Pallas kernels, per_device(): return associate(sent, keep(ordered), windows)[0]  5.11 us
    all_to_all x1, waiting for transfers between devices, per_device(): library = lax.all_to_all(library, 'gene', 0, 0, tiled=True)  4.41 us
    pallas_call x1, Pallas kernels, per_device(): sums, = sum_cells(parts)  2.91 us
    pallas_call x1, Pallas kernels, per_device(): ordered, = order_dosage(dosage)  1.72 us
  transfers between devices with their start and end apart: 2, of which 2 were waited for; matrix products, arithmetic and copies ran while one was open for 0% of the time, Pallas kernels for 7%

profile of v4, /device:TPU:1, one launch (start us, length us, event | category | flops | bytes accessed | tf_op | source)
XLA Modules:
  0.0 67.1 jit_solution(7966268515046978434)
XLA Ops:
  0.0 1.5 %pack.1 = f32[8,144,128]{2,1,0:T(8,128)S(1)} custom-call(s32[512,256]{1,0:T(8,128)} %counts_hbm.1, s32[4,128]{1,0:T(4,128)} %bitcast.2, s32[4,128]{1,0:T(4,128)} %bitcast.3, f32[8,50]{1,0:T(8,128)} %cov_hbm.1), custom_call_target="tpu_custom_call" | custom-call | tf_op jit(solution)/shard_map/pack/pallas_call | solution.py:366
  1.6 0.0 copy-start
  1.6 28.2 %all_to_all.15.part_ref = f32[8,144,128]{2,1,0:T(8,128)S(1)} all-to-all(f32[8,144,128]{2,1,0:T(8,128)S(1)} %pack.1), channel_id=1, replica_groups=mesh['cell'=8,'donor'=8,'gene'=8] {'cell'}, dimensions={0} | all-to-all | bytes 1179648 | tf_op jit(solution)/shard_map/all_to_all | solution.py:372
  29.8 1.1 %sum_library.1 = f32[8,16,128]{2,1,0:T(8,128)} custom-call(f32[8,144,128]{2,1,0:T(8,128)S(1)} %all_to_all.15.part_ref), custom_call_target="tpu_custom_call" | custom-call | tf_op jit(solution)/shard_map/sum_library/pallas_call | solution.py:374
  31.0 6.8 %all-to-all-start.1 = ((f32[8,16,128]{2,1,0:T(8,128)}), f32[8,16,128]{2,1,0:T(8,128)S(1)}, u32[]{:S(2)}, u32[]{:S(2)}) async-start(f32[8,16,128]{2,1,0:T(8,128)} %sum_library.1), calls=%async_computation.1 | async-start | bytes 131072 | tf_op jit(solution)/shard_map/all_to_all | solution.py:375
  37.8 2.9 %sum_cells.1.sum_hbm = f32[384,128]{1,0:T(8,128)} custom-call(f32[8,144,128]{2,1,0:T(8,128)S(1)} %all_to_all.15.part_ref), custom_call_target="tpu_custom_call" | custom-call | tf_op jit(solution)/shard_map/sum_cells/pallas_call | solution.py:376
  40.7 4.4 %all-to-all-done.1.library_ref = f32[8,16,128]{2,1,0:T(8,128)S(1)} async-done(((f32[8,16,128]{2,1,0:T(8,128)}), f32[8,16,128]{2,1,0:T(8,128)S(1)}, u32[]{:S(2)}, u32[]{:S(2)}) %all-to-all-start.1) | async-done | bytes 65568 | tf_op jit(solution)/shard_map/all_to_all | solution.py:375
  45.1 1.7 %express.1 = f32[8,80,128]{2,1,0:T(8,128)} custom-call(f32[8,144,128]{2,1,0:T(8,128)S(1)} %all_to_all.15.part_ref, f32[384,128]{1,0:T(8,128)} %sum_cells.1.sum_hbm, f32[8,16,128]{2,1,0:T(8,128)S(1)} %all-to-all-done.1.library_ref), custom_call_target="tpu_custom_call" | custom-call | tf_op jit(solution)/shard_map/express/pallas_call | solution.py:377
  46.8 0.0 copy-start.1
  46.9 8.0 %all-to-all-start.2 = ((f32[8,80,128]{2,1,0:T(8,128)}), f32[8,80,128]{2,1,0:T(8,128)S(1)}, u32[]{:S(2)}, u32[]{:S(2)}) async-start(f32[8,80,128]{2,1,0:T(8,128)} %express.1), calls=%async_computation.2 | async-start | bytes 655360 | tf_op jit(solution)/shard_map/all_to_all | solution.py:378
  54.9 0.0 copy-done
  54.9 1.7 %order_dosage.1.dosage_hbm = bf16[1024,512]{1,0:T(8,128)(2,1)} custom-call(s32[1024,512]{1,0:T(8,128)S(1)} %copy-done), custom_call_target="tpu_custom_call" | custom-call | tf_op jit(solution)/shard_map/order_dosage/pallas_call | solution.py:373
  56.6 5.4 %all-to-all-done.2.recv_ref = f32[8,80,128]{2,1,0:T(8,128)S(1)} async-done(((f32[8,80,128]{2,1,0:T(8,128)}), f32[8,80,128]{2,1,0:T(8,128)S(1)}, u32[]{:S(2)}, u32[]{:S(2)}) %all-to-all-start.2) | async-done | bytes 327712 | tf_op jit(solution)/shard_map/all_to_all | solution.py:378
  62.0 0.0 copy-done.1
  62.0 5.1 %associate.1 = f32[24,4,1024]{2,1,0:T(4,128)} custom-call(f32[8,80,128]{2,1,0:T(8,128)S(1)} %all-to-all-done.2.recv_ref, bf16[1024,512]{1,0:T(8,128)(2,1)} %order_dosage.1.dosage_hbm, s32[4,1024]{1,0:T(4,128)S(1)} %copy-done.1), custom_call_target="tpu_custom_call" | custom-call | tf_op jit(solution)/shard_map/associate/pallas_call | solution.py:379
Async XLA Ops:
  1.6 53.3 %copy-start = (s32[1024,512]{1,0:T(8,128)S(1)}, s32[1024,512]{1,0:T(8,128)}, u32[]{:S(2)}) copy-start(s32[1024,512]{1,0:T(8,128)} %dosage_ref.1) | copy-start | bytes 6291460
  31.0 14.2 %all-to-all-start.1 = ((f32[8,16,128]{2,1,0:T(8,128)}), f32[8,16,128]{2,1,0:T(8,128)S(1)}, u32[]{:S(2)}, u32[]{:S(2)}) async-start(f32[8,16,128]{2,1,0:T(8,128)} %sum_library.1), calls=%async_computation.1 | async-start | bytes 131072 | tf_op jit(solution)/shard_map/all_to_all | solution.py:375
  46.8 15.2 %copy-start.1 = (s32[4,1024]{1,0:T(4,128)S(1)}, s32[4,1024]{1,0:T(4,128)}, u32[]{:S(2)}) copy-start(s32[4,1024]{1,0:T(4,128)} %windows_ref.1) | copy-start | bytes 49156
  46.9 15.2 %all-to-all-start.2 = ((f32[8,80,128]{2,1,0:T(8,128)}), f32[8,80,128]{2,1,0:T(8,128)S(1)}, u32[]{:S(2)}, u32[]{:S(2)}) async-start(f32[8,80,128]{2,1,0:T(8,128)} %express.1), calls=%async_computation.2 | async-start | bytes 655360 | tf_op jit(solution)/shard_map/all_to_all | solution.py:378

commit v5 on v4

--- a/solution.py
+++ b/solution.py
@@ -37,7 +37,7 @@
 SUM_ROWS = HALF * GENE_PART
 LIB_ROWS = 16
 EXPR_ROWS = HALF * OWN
-SEND_ROWS = EXPR_ROWS + N * N // 2
+SEND_ROWS = EXPR_ROWS + DON_GRP // 2
 
 NT = (((1,), (1,)), ((), ()))
 PLAIN = (((1,), (0,)), ((), ()))
@@ -122,10 +122,21 @@
         copy.wait()
 
 
-def sum_kernel(part_ref, sum_hbm, sum_ref, sem):
-    sum_ref[...] = jnp.zeros_like(sum_ref)
-
-    def one_block(block, carry):
+def sum_kernel(part_ref, out_hbm, sum_ref, out_ref, sems):
+    lane = lax.broadcasted_iota(I32, (SUB, LANES), 1)
+    first_half = lax.broadcasted_iota(I32, (SUB, LANES), 0) < N // 2
+    tiles = []
+    for cell in range(N):
+        tile = part_ref[cell, TOTAL_ROW:PART_ROWS, :]
+        tile = jnp.where(first_half, pltpu.roll(tile, N // 2, 0), pltpu.roll(tile, DON_GRP, 1))
+        tiles.append(jnp.where(lane < NCOV, tile, jnp.where(lane == NCOV, 1.0, 0.0)))
+    tiles.append(jnp.zeros((DON_GRP, LANES), F32))
+    turned = jnp.concatenate(tiles, axis=0).T
+    design = turned[: DON_GRP // 2] + pltpu.roll(turned[DON_GRP // 2 : DON_GRP], DON_GRP, 1)
+    for peer in range(N):
+        out_ref[peer, EXPR_ROWS:, :] = design
+
+    def one_block(block):
         onehot, step = read_labels(part_ref, block)
         counts = jnp.concatenate(
             [
@@ -139,47 +150,69 @@
             [jnp.where(step == number, counts, 0.0).astype(BF16) for number in range(HALF)],
             axis=0,
         )
-        sum_ref[...] += lax.dot_general(left, onehot, NT, preferred_element_type=F32)
-        return carry
-
-    lax.fori_loop(0, N, one_block, 0)
-    copy = pltpu.make_async_copy(sum_ref, sum_hbm, sem)
-    copy.start()
-    copy.wait()
-
-
-def expression_kernel(part_ref, sum_hbm, library_ref, out_ref, sum_ref, sem):
-    copy = pltpu.make_async_copy(sum_hbm, sum_ref, sem)
-    copy.start()
-    for cell in range(N):
-        row = EXPR_ROWS + cell * (N // 2)
-        packed = part_ref[cell, COV_ROW:PART_ROWS, :]
+        return lax.dot_general(left, onehot, NT, preferred_element_type=F32)
+
+    for block in range(0, N, 2):
+        added = one_block(block) + one_block(block + 1)
+        if block == 0:
+            sum_ref[...] = added
+        else:
+            sum_ref[...] += added
+    for step in range(HALF):
+        logs = jnp.log2(sum_ref[step * GENE_PART : (step + 1) * GENE_PART, :] + 0.5)
         for peer in range(N):
-            out_ref[peer, row : row + N // 2, :] = packed
+            out_ref[peer, step * OWN : (step + 1) * OWN, :] = logs[peer * OWN : (peer + 1) * OWN]
+    copy_all([(out_ref.at[peer], out_hbm.at[peer]) for peer in range(N)], sems)
+
+
+def copy_all(pairs, sems):
+    copies = [
+        pltpu.make_async_copy(source, target, sems.at[index])
+        for index, (source, target) in enumerate(pairs)
+    ]
+    for copy in copies:
+        copy.start()
+    for copy in copies:
+        copy.wait()
+
+
+def expression_kernel(sent_hbm, library_ref, out_hbm, sent_ref, in_sems, out_sems):
+    logs = pl.ds(0, EXPR_ROWS)
+    arrivals = [
+        pltpu.make_async_copy(sent_hbm.at[peer, logs], sent_ref.at[peer], in_sems.at[peer])
+        for peer in range(N)
+    ]
+    for copy in arrivals:
+        copy.start()
     library = library_ref[0]
     for peer in range(1, N):
         library = library + library_ref[peer]
-    library = library + 1.0
-    copy.wait()
-    for step in range(HALF):
-        summed = sum_ref[step * GENE_PART : (step + 1) * GENE_PART, :]
-        expression = jnp.log2((summed + 0.5) / library[step : step + 1] * 1000000.0)
-        for peer in range(N):
-            out_ref[peer, step * OWN : (step + 1) * OWN, :] = expression[
-                peer * OWN : (peer + 1) * OWN
-            ]
+    shift = math.log2(1000000.0) - jnp.log2(library + 1.0)
+    shift = jnp.concatenate(
+        [jnp.broadcast_to(shift[step : step + 1], (OWN, LANES)) for step in range(HALF)], axis=0
+    )
+    departures = []
+    for peer in range(N):
+        arrivals[peer].wait()
+        sent_ref[peer] += shift
+        departures.append(
+            pltpu.make_async_copy(sent_ref.at[peer], out_hbm.at[peer, logs], out_sems.at[peer])
+        )
+        departures[peer].start()
+    for copy in departures:
+        copy.wait()
 
 
 def dosage_kernel(dosage_ref, out_hbm, out_ref, sem):
-    row = lax.broadcasted_iota(I32, (DONORS, DONORS), 0)
-    place = lax.broadcasted_iota(I32, (1, DONORS), 1)
+    place = lax.broadcasted_iota(I32, (DONORS, 1), 0)
+    column = lax.broadcasted_iota(I32, (DONORS, DONORS), 1)
     source = (((place >> 3) & 7) << 6) + ((place >> 6) << 3) + (place & 7)
-    order = jnp.where(row == source, 1.0, 0.0).astype(BF16)
+    order = jnp.where(column == source, 1.0, 0.0).astype(BF16)
     span = 256
     for start in range(0, SNPS, span):
         half = dosage_ref[start : start + span, :].astype(F32).astype(BF16)
-        moved = lax.dot_general(half, order, PLAIN, preferred_element_type=F32)
-        out_ref[start : start + span, :] = moved.astype(BF16)
+        moved = lax.dot_general(order, half, NT, preferred_element_type=F32)
+        out_ref[:, start : start + span] = moved.astype(BF16)
     copy = pltpu.make_async_copy(out_ref, out_hbm, sem)
     copy.start()
     copy.wait()
@@ -190,20 +223,41 @@
 ):
     copy = pltpu.make_async_copy(dosage_hbm, dosage_ref, sem)
     copy.start()
-    lane = lax.broadcasted_iota(I32, (SUB, LANES), 1)
-    first_half = lax.broadcasted_iota(I32, (SUB, LANES), 0) < N // 2
-    tiles = []
-    for donor in range(N):
-        for pair in range(N // 2):
-            row = EXPR_ROWS + pair * SUB
-            tile = recv_ref[donor, row : row + SUB, :]
-            other = pltpu.roll(tile, DON_GRP, 1)
-            tiles.append(jnp.where(first_half, tile, pltpu.roll(other, N // 2, 0)))
-            tiles.append(jnp.where(first_half, pltpu.roll(tile, N // 2, 0), other))
-    ends = jnp.where(lane == NCOV, 1.0, 0.0)
-    design = jnp.concatenate([jnp.where(lane < NCOV, tile, ends) for tile in tiles], axis=0)
-    turned = design.T
-    gram = lax.dot_general(turned, turned, NT, precision=HIGHEST, preferred_element_type=F32)
+    half_rows = DON_GRP // 2
+    lane = lax.broadcasted_iota(I32, (half_rows, LANES), 1)
+    lower, upper = [], []
+    for pair in range(N // 2):
+        one, two = recv_ref[2 * pair, EXPR_ROWS:, :], recv_ref[2 * pair + 1, EXPR_ROWS:, :]
+        lower.append(jnp.where(lane < DON_GRP, one, pltpu.roll(two, DON_GRP, 1)))
+        upper.append(jnp.where(lane < DON_GRP, pltpu.roll(one, DON_GRP, 1), two))
+    turned = jnp.concatenate(
+        [jnp.concatenate(lower, axis=1), jnp.concatenate(upper, axis=1)], axis=0
+    )
+    padded = jnp.concatenate([turned, jnp.zeros_like(turned)], axis=0)
+    wide_lane = lax.broadcasted_iota(I32, (EXPR_ROWS, LANES), 1)
+    for pair in range(N // 2):
+        one, two = recv_ref[2 * pair, :EXPR_ROWS, :], recv_ref[2 * pair + 1, :EXPR_ROWS, :]
+        expression_ref[pair, :EXPR_ROWS, :] = jnp.where(
+            wide_lane < DON_GRP, one, pltpu.roll(two, DON_GRP, 1)
+        )
+        expression_ref[pair, EXPR_ROWS:, :] = jnp.where(
+            wide_lane < DON_GRP, pltpu.roll(one, DON_GRP, 1), two
+        )
+    expression = jnp.concatenate(
+        [
+            jnp.concatenate(
+                [
+                    expression_ref[pair, pl.ds(gene, CT, stride=OWN), :]
+                    for gene in range(OWN)
+                ],
+                axis=0,
+            )
+            for pair in range(N // 2)
+        ],
+        axis=1,
+    )
+    cross = lax.dot_general(expression, padded, NT, precision=HIGHEST, preferred_element_type=F32)
+    gram = lax.dot_general(turned, padded, NT, precision=HIGHEST, preferred_element_type=F32)
     rows = ORDER_ROWS
     row_id = lax.broadcasted_iota(I32, (rows, LANES), 0)
     lane_id = lax.broadcasted_iota(I32, (rows, LANES), 1)
@@ -225,32 +279,12 @@
     scale = 1.0 / jnp.sqrt(jnp.where(row_col < ORDER, pivots, 1.0))
     inverse = pltpu.roll(work, 64, 1)
     inverse = jnp.where((lane_id < ORDER) & (row_id < ORDER), inverse * scale, 0.0)
-    basis = lax.dot_general(inverse, turned, PLAIN, precision=HIGHEST, preferred_element_type=F32)
-    wide_lane = lax.broadcasted_iota(I32, (EXPR_ROWS, LANES), 1)
-    for pair in range(N // 2):
-        one, two = recv_ref[2 * pair, :EXPR_ROWS, :], recv_ref[2 * pair + 1, :EXPR_ROWS, :]
-        expression_ref[pair, :EXPR_ROWS, :] = jnp.where(
-            wide_lane < DON_GRP, one, pltpu.roll(two, DON_GRP, 1)
-        )
-        expression_ref[pair, EXPR_ROWS:, :] = jnp.where(
-            wide_lane < DON_GRP, pltpu.roll(one, DON_GRP, 1), two
-        )
-    expression = jnp.concatenate(
-        [
-            jnp.concatenate(
-                [
-                    expression_ref[pair, pl.ds(gene, CT, stride=OWN), :]
-                    for gene in range(OWN)
-                ],
-                axis=0,
-            )
-            for pair in range(N // 2)
-        ],
-        axis=1,
-    )
-    fit = lax.dot_general(expression, basis, NT, precision=HIGHEST, preferred_element_type=F32)
+    half_way = lax.dot_general(cross, inverse, NT, precision=HIGHEST, preferred_element_type=F32)
+    coefficients = lax.dot_general(
+        half_way, inverse, PLAIN, precision=HIGHEST, preferred_element_type=F32
+    )
     residual = expression - lax.dot_general(
-        fit, basis, PLAIN, precision=HIGHEST, preferred_element_type=F32
+        coefficients, padded, PLAIN, precision=HIGHEST, preferred_element_type=F32
     )
     upper_part = residual.astype(BF16)
     lower_part = (residual - upper_part.astype(F32)).astype(BF16)
@@ -258,7 +292,7 @@
     products = lax.dot_general(
         jnp.concatenate([upper_part, lower_part], axis=0),
         dosage_ref[...],
-        NT,
+        PLAIN,
         preferred_element_type=F32,
     )
     both = OWN * CT
@@ -282,7 +316,7 @@
 VMEM = pl.BlockSpec(memory_space=pltpu.VMEM)
 
 
-def call(kernel, name, outs, ins, limit, scratch=()):
+def call(kernel, name, outs, ins, limit, scratch=(), aliases=None):
     return pl.pallas_call(
         kernel,
         name=name,
@@ -290,6 +324,7 @@
         in_specs=ins,
         out_specs=[spec for _, spec in outs],
         scratch_shapes=scratch,
+        input_output_aliases=aliases or {},
         compiler_params=pltpu.CompilerParams(vmem_limit_bytes=limit * MIB),
     )
 
@@ -298,7 +333,7 @@
 SUM_SHAPE = (SUM_ROWS, LANES)
 LIBRARY_SHAPE = (N, LIB_ROWS, LANES)
 SEND_SHAPE = (N, SEND_ROWS, LANES)
-DOSAGE_SHAPE = (SNPS, DONORS)
+DOSAGE_SHAPE = (DONORS, SNPS)
 DMA = pltpu.SemaphoreType.DMA
 
 pack = call(
@@ -327,18 +362,19 @@
 sum_cells = call(
     sum_kernel,
     "sum_cells",
-    [(pltpu.HBM(SUM_SHAPE, F32), HBM)],
+    [(pltpu.HBM(SEND_SHAPE, F32), HBM)],
     [VMEM],
     16,
-    [pltpu.VMEM(SUM_SHAPE, F32), DMA],
+    [pltpu.VMEM(SUM_SHAPE, F32), pltpu.VMEM(SEND_SHAPE, F32), DMA((N,))],
 )
 express = call(
     expression_kernel,
     "express",
-    [(jax.ShapeDtypeStruct(SEND_SHAPE, F32), VMEM)],
-    [VMEM, HBM, VMEM],
+    [(pltpu.HBM(SEND_SHAPE, F32), HBM)],
+    [HBM, VMEM],
     8,
-    [pltpu.VMEM(SUM_SHAPE, F32), DMA],
+    [pltpu.VMEM((N, EXPR_ROWS, LANES), F32), DMA((N,)), DMA((N,))],
+    {0: 0},
 )
 order_dosage = call(
     dosage_kernel,
@@ -373,8 +409,8 @@
     (ordered,) = order_dosage(dosage)
     (library,) = sum_library(parts)
     library = lax.all_to_all(library, "gene", 0, 0, tiled=True)
-    (sums,) = sum_cells(parts)
-    (sent,) = express(parts, keep(sums), library)
+    (sent,) = sum_cells(parts)
+    (sent,) = express(keep(sent), library)
     sent = lax.all_to_all(sent, "donor", 0, 0, tiled=True)
     return associate(sent, keep(ordered), windows)[0]
 

time: 67.6 us -> 66.8 us (0.988)
  Pallas kernels: 14.1 us -> 12.3 us
  waiting for transfers between devices: 9.8 us -> 10.9 us
    pallas_call x2, Pallas kernels: 4.62 us -> 3.39 us  [the longest x1 1.78 us: per_device(): sent, = sum_cells(parts)]
    all_to_all x1, waiting for transfers between devices: 4.41 us -> 5.53 us  [per_device(): library = lax.all_to_all(library, 'gene', 0, 0, tiled=True)]
  transfers between devices with their start and end apart: 2 -> 2, of which waited for: 2 -> 2; matrix products, arithmetic and copies ran while one was open for 0% -> 0% of each run, Pallas kernels for 7% -> 5%
where the time goes in v5:
time: 66.8 us; the launch traced here: 66.4 us
  blocking collectives  28.2 us (42%)
  starting transfers between devices  14.9 us (22%)
  Pallas kernels  12.3 us (18%)
  waiting for transfers between devices  10.9 us (16%)
    all_to_all x1, blocking collectives, per_device(): parts = lax.all_to_all(parts, 'cell', 0, 0, tiled=True)  28.2 us
    all_to_all x1, starting transfers between devices, per_device(): sent = lax.all_to_all(sent, 'donor', 0, 0, tiled=True)  8.05 us
    all_to_all x1, starting transfers between devices, per_device(): library = lax.all_to_all(library, 'gene', 0, 0, tiled=True)  6.83 us
    all_to_all x1, waiting for transfers between devices, per_device(): library = lax.all_to_all(library, 'gene', 0, 0, tiled=True)  5.53 us
    all_to_all x1, waiting for transfers between devices, per_device(): sent = lax.all_to_all(sent, 'donor', 0, 0, tiled=True)  5.37 us
    pallas_call x1, Pallas kernels, per_device(): return associate(sent, keep(ordered), windows)[0]  4.47 us
    pallas_call x1, Pallas kernels, per_device(): sent, = sum_cells(parts)  1.78 us
    pallas_call x1, Pallas kernels, per_device(): ordered, = order_dosage(dosage)  1.74 us
  transfers between devices with their start and end apart: 2, of which 2 were waited for; matrix products, arithmetic and copies ran while one was open for 0% of the time, Pallas kernels for 5%

profile of v5, /device:TPU:1, one launch (start us, length us, event | category | flops | bytes accessed | tf_op | source)
XLA Modules:
  0.0 66.4 jit_solution(109262994095316286)
XLA Ops:
  0.0 1.5 %pack.1 = f32[8,144,128]{2,1,0:T(8,128)S(1)} custom-call(s32[512,256]{1,0:T(8,128)} %counts_hbm.1, s32[4,128]{1,0:T(4,128)} %bitcast.2, s32[4,128]{1,0:T(4,128)} %bitcast.3, f32[8,50]{1,0:T(8,128)} %cov_hbm.1), custom_call_target="tpu_custom_call" | custom-call | tf_op jit(solution)/shard_map/pack/pallas_call | solution.py:402
  1.6 0.0 copy-start
  1.6 28.2 %all_to_all.15.part_ref = f32[8,144,128]{2,1,0:T(8,128)S(1)} all-to-all(f32[8,144,128]{2,1,0:T(8,128)S(1)} %pack.1), channel_id=1, replica_groups=mesh['cell'=8,'donor'=8,'gene'=8] {'cell'}, dimensions={0} | all-to-all | bytes 1179648 | tf_op jit(solution)/shard_map/all_to_all | solution.py:408
  29.8 1.1 %sum_library.1 = f32[8,16,128]{2,1,0:T(8,128)} custom-call(f32[8,144,128]{2,1,0:T(8,128)S(1)} %all_to_all.15.part_ref), custom_call_target="tpu_custom_call" | custom-call | tf_op jit(solution)/shard_map/sum_library/pallas_call | solution.py:410
  31.0 6.8 %all-to-all-start.1 = ((f32[8,16,128]{2,1,0:T(8,128)}), f32[8,16,128]{2,1,0:T(8,128)S(1)}, u32[]{:S(2)}, u32[]{:S(2)}) async-start(f32[8,16,128]{2,1,0:T(8,128)} %sum_library.1), calls=%async_computation.1 | async-start | bytes 131072 | tf_op jit(solution)/shard_map/all_to_all | solution.py:411
  37.8 1.8 %sum_cells.1.sent_hbm = f32[8,80,128]{2,1,0:T(8,128)} custom-call(f32[8,144,128]{2,1,0:T(8,128)S(1)} %all_to_all.15.part_ref), custom_call_target="tpu_custom_call" | custom-call | tf_op jit(solution)/shard_map/sum_cells/pallas_call | solution.py:412
  39.6 0.0 copy-start.1
  39.6 5.5 %all-to-all-done.1.library_ref = f32[8,16,128]{2,1,0:T(8,128)S(1)} async-done(((f32[8,16,128]{2,1,0:T(8,128)}), f32[8,16,128]{2,1,0:T(8,128)S(1)}, u32[]{:S(2)}, u32[]{:S(2)}) %all-to-all-start.1) | async-done | bytes 65568 | tf_op jit(solution)/shard_map/all_to_all | solution.py:411
  45.1 1.6 %express.1 = f32[8,80,128]{2,1,0:T(8,128)} custom-call(f32[8,80,128]{2,1,0:T(8,128)} %sum_cells.1.sent_hbm, f32[8,16,128]{2,1,0:T(8,128)S(1)} %all-to-all-done.1.library_ref), custom_call_target="tpu_custom_call", output_to_operand_aliasing={{}: (0, {})} | custom-call | tf_op jit(solution)/shard_map/express/pallas_call | solution.py:413
  46.7 8.0 %all-to-all-start.2 = ((f32[8,80,128]{2,1,0:T(8,128)}), f32[8,80,128]{2,1,0:T(8,128)S(1)}, u32[]{:S(2)}, u32[]{:S(2)}) async-start(f32[8,80,128]{2,1,0:T(8,128)} %express.1), calls=%async_computation.2 | async-start | bytes 655360 | tf_op jit(solution)/shard_map/all_to_all | solution.py:414
  54.8 0.0 copy-done
  54.8 1.7 %order_dosage.1.dosage_hbm = bf16[512,1024]{1,0:T(8,128)(2,1)} custom-call(s32[1024,512]{1,0:T(8,128)S(1)} %copy-done), custom_call_target="tpu_custom_call" | custom-call | tf_op jit(solution)/shard_map/order_dosage/pallas_call | solution.py:409
  56.5 5.4 %all-to-all-done.2.recv_ref = f32[8,80,128]{2,1,0:T(8,128)S(1)} async-done(((f32[8,80,128]{2,1,0:T(8,128)}), f32[8,80,128]{2,1,0:T(8,128)S(1)}, u32[]{:S(2)}, u32[]{:S(2)}) %all-to-all-start.2) | async-done | bytes 327712 | tf_op jit(solution)/shard_map/all_to_all | solution.py:414
  61.9 0.0 copy-done.1
  61.9 4.5 %associate.1 = f32[24,4,1024]{2,1,0:T(4,128)} custom-call(f32[8,80,128]{2,1,0:T(8,128)S(1)} %all-to-all-done.2.recv_ref, bf16[512,1024]{1,0:T(8,128)(2,1)} %order_dosage.1.dosage_hbm, s32[4,1024]{1,0:T(4,128)S(1)} %copy-done.1), custom_call_target="tpu_custom_call" | custom-call | tf_op jit(solution)/shard_map/associate/pallas_call | solution.py:415
Async XLA Ops:
  1.6 53.2 %copy-start = (s32[1024,512]{1,0:T(8,128)S(1)}, s32[1024,512]{1,0:T(8,128)}, u32[]{:S(2)}) copy-start(s32[1024,512]{1,0:T(8,128)} %dosage_ref.1) | copy-start | bytes 6291460
  31.0 14.2 %all-to-all-start.1 = ((f32[8,16,128]{2,1,0:T(8,128)}), f32[8,16,128]{2,1,0:T(8,128)S(1)}, u32[]{:S(2)}, u32[]{:S(2)}) async-start(f32[8,16,128]{2,1,0:T(8,128)} %sum_library.1), calls=%async_computation.1 | async-start | bytes 131072 | tf_op jit(solution)/shard_map/all_to_all | solution.py:411
  39.6 22.3 %copy-start.1 = (s32[4,1024]{1,0:T(4,128)S(1)}, s32[4,1024]{1,0:T(4,128)}, u32[]{:S(2)}) copy-start(s32[4,1024]{1,0:T(4,128)} %windows_ref.1) | copy-start | bytes 49156
  46.7 15.2 %all-to-all-start.2 = ((f32[8,80,128]{2,1,0:T(8,128)}), f32[8,80,128]{2,1,0:T(8,128)S(1)}, u32[]{:S(2)}, u32[]{:S(2)}) async-start(f32[8,80,128]{2,1,0:T(8,128)} %express.1), calls=%async_computation.2 | async-start | bytes 655360 | tf_op jit(solution)/shard_map/all_to_all | solution.py:414

commit v6 on v5

--- a/solution.py
+++ b/solution.py
@@ -29,6 +29,8 @@
 DONORS = N * DON_GRP
 SNPS = 1024
 WIN = 1024
+SPAN = 256
+PIECE = 64
 DONOR_ROW = CHUNKS * GENE_PART
 TYPE_ROW = DONOR_ROW + CHUNKS
 TOTAL_ROW = TYPE_ROW + CHUNKS
@@ -111,7 +113,9 @@
         summed = summed + lax.dot_general(
             left.astype(BF16), onehot, NT, preferred_element_type=F32
         )
-    library_ref[...] = summed[:LIB_ROWS] + summed[LIB_ROWS:]
+    summed = summed[:LIB_ROWS] + summed[LIB_ROWS:]
+    for group in range(HALF // OWN):
+        library_ref[group] = summed[group * OWN : (group + 1) * OWN]
     copies = [
         pltpu.make_async_copy(library_ref, library_hbm.at[peer], sems.at[peer])
         for peer in range(N)
@@ -122,7 +126,9 @@
         copy.wait()
 
 
-def sum_kernel(part_ref, out_hbm, sum_ref, out_ref, sems):
+def prepare_kernel(
+    part_ref, dosage_ref, out_hbm, ordered_hbm, sum_ref, out_ref, ordered_ref, sems
+):
     lane = lax.broadcasted_iota(I32, (SUB, LANES), 1)
     first_half = lax.broadcasted_iota(I32, (SUB, LANES), 0) < N // 2
     tiles = []
@@ -162,24 +168,34 @@
         logs = jnp.log2(sum_ref[step * GENE_PART : (step + 1) * GENE_PART, :] + 0.5)
         for peer in range(N):
             out_ref[peer, step * OWN : (step + 1) * OWN, :] = logs[peer * OWN : (peer + 1) * OWN]
-    copy_all([(out_ref.at[peer], out_hbm.at[peer]) for peer in range(N)], sems)
-
-
-def copy_all(pairs, sems):
     copies = [
-        pltpu.make_async_copy(source, target, sems.at[index])
-        for index, (source, target) in enumerate(pairs)
+        pltpu.make_async_copy(out_ref.at[peer], out_hbm.at[peer], sems.at[peer])
+        for peer in range(N)
     ]
     for copy in copies:
         copy.start()
+    place = lax.broadcasted_iota(I32, (DONORS, 1), 0)
+    column = lax.broadcasted_iota(I32, (DONORS, DONORS), 1)
+    source = (((place >> 3) & 7) << 6) + ((place >> 6) << 3) + (place & 7)
+    order = jnp.where(column == source, 1.0, 0.0).astype(BF16)
+    for index in range(SNPS // SPAN):
+        span = pl.ds(index * SPAN, SPAN)
+        half = dosage_ref[span, :].astype(F32).astype(BF16)
+        moved = lax.dot_general(order, half, NT, preferred_element_type=F32)
+        ordered_ref[:, span] = moved.astype(BF16)
+        copies.append(
+            pltpu.make_async_copy(
+                ordered_ref.at[:, span], ordered_hbm.at[:, span], sems.at[N + index]
+            )
+        )
+        copies[-1].start()
     for copy in copies:
         copy.wait()
 
 
-def expression_kernel(sent_hbm, library_ref, out_hbm, sent_ref, in_sems, out_sems):
-    logs = pl.ds(0, EXPR_ROWS)
+def expression_kernel(sent_hbm, library_ref, out_ref, sems):
     arrivals = [
-        pltpu.make_async_copy(sent_hbm.at[peer, logs], sent_ref.at[peer], in_sems.at[peer])
+        pltpu.make_async_copy(sent_hbm.at[peer], out_ref.at[peer], sems.at[peer])
         for peer in range(N)
     ]
     for copy in arrivals:
@@ -189,40 +205,31 @@
         library = library + library_ref[peer]
     shift = math.log2(1000000.0) - jnp.log2(library + 1.0)
     shift = jnp.concatenate(
-        [jnp.broadcast_to(shift[step : step + 1], (OWN, LANES)) for step in range(HALF)], axis=0
-    )
-    departures = []
+        [
+            jnp.broadcast_to(shift[group, row : row + 1], (OWN, LANES))
+            for group in range(HALF // OWN)
+            for row in range(OWN)
+        ],
+        axis=0,
+    )
     for peer in range(N):
         arrivals[peer].wait()
-        sent_ref[peer] += shift
-        departures.append(
-            pltpu.make_async_copy(sent_ref.at[peer], out_hbm.at[peer, logs], out_sems.at[peer])
-        )
-        departures[peer].start()
-    for copy in departures:
-        copy.wait()
-
-
-def dosage_kernel(dosage_ref, out_hbm, out_ref, sem):
-    place = lax.broadcasted_iota(I32, (DONORS, 1), 0)
-    column = lax.broadcasted_iota(I32, (DONORS, DONORS), 1)
-    source = (((place >> 3) & 7) << 6) + ((place >> 6) << 3) + (place & 7)
-    order = jnp.where(column == source, 1.0, 0.0).astype(BF16)
-    span = 256
-    for start in range(0, SNPS, span):
-        half = dosage_ref[start : start + span, :].astype(F32).astype(BF16)
-        moved = lax.dot_general(order, half, NT, preferred_element_type=F32)
-        out_ref[:, start : start + span] = moved.astype(BF16)
-    copy = pltpu.make_async_copy(out_ref, out_hbm, sem)
-    copy.start()
-    copy.wait()
+        out_ref[peer, :EXPR_ROWS, :] += shift
 
 
 def association_kernel(
-    recv_ref, dosage_hbm, windows_ref, out_ref, dosage_ref, expression_ref, sem
+    recv_ref, dosage_hbm, windows_ref, out_ref, dosage_ref, expression_ref, sems
 ):
-    copy = pltpu.make_async_copy(dosage_hbm, dosage_ref, sem)
-    copy.start()
+    copies = [
+        pltpu.make_async_copy(
+            dosage_hbm.at[pl.ds(start, PIECE)],
+            dosage_ref.at[pl.ds(start, PIECE)],
+            sems.at[start // PIECE],
+        )
+        for start in range(0, DONORS, PIECE)
+    ]
+    for copy in copies:
+        copy.start()
     half_rows = DON_GRP // 2
     lane = lax.broadcasted_iota(I32, (half_rows, LANES), 1)
     lower, upper = [], []
@@ -288,7 +295,8 @@
     )
     upper_part = residual.astype(BF16)
     lower_part = (residual - upper_part.astype(F32)).astype(BF16)
-    copy.wait()
+    for copy in copies:
+        copy.wait()
     products = lax.dot_general(
         jnp.concatenate([upper_part, lower_part], axis=0),
         dosage_ref[...],
@@ -331,7 +339,7 @@
 
 PART_SHAPE = (N, PART_ROWS, LANES)
 SUM_SHAPE = (SUM_ROWS, LANES)
-LIBRARY_SHAPE = (N, LIB_ROWS, LANES)
+LIBRARY_SHAPE = (N, HALF // OWN, OWN, LANES)
 SEND_SHAPE = (N, SEND_ROWS, LANES)
 DOSAGE_SHAPE = (DONORS, SNPS)
 DMA = pltpu.SemaphoreType.DMA
@@ -359,30 +367,26 @@
     8,
     [pltpu.VMEM(LIBRARY_SHAPE[1:], F32), DMA((N,))],
 )
-sum_cells = call(
-    sum_kernel,
-    "sum_cells",
-    [(pltpu.HBM(SEND_SHAPE, F32), HBM)],
-    [VMEM],
+prepare = call(
+    prepare_kernel,
+    "prepare",
+    [(pltpu.HBM(SEND_SHAPE, F32), HBM), (pltpu.HBM(DOSAGE_SHAPE, BF16), HBM)],
+    [VMEM, VMEM],
     16,
-    [pltpu.VMEM(SUM_SHAPE, F32), pltpu.VMEM(SEND_SHAPE, F32), DMA((N,))],
+    [
+        pltpu.VMEM(SUM_SHAPE, F32),
+        pltpu.VMEM(SEND_SHAPE, F32),
+        pltpu.VMEM(DOSAGE_SHAPE, BF16),
+        DMA((N + SNPS // SPAN,)),
+    ],
 )
 express = call(
     expression_kernel,
     "express",
-    [(pltpu.HBM(SEND_SHAPE, F32), HBM)],
+    [(jax.ShapeDtypeStruct(SEND_SHAPE, F32), VMEM)],
     [HBM, VMEM],
     8,
-    [pltpu.VMEM((N, EXPR_ROWS, LANES), F32), DMA((N,)), DMA((N,))],
-    {0: 0},
-)
-order_dosage = call(
-    dosage_kernel,
-    "order_dosage",
-    [(pltpu.HBM(DOSAGE_SHAPE, BF16), HBM)],
-    [VMEM],
-    16,
-    [pltpu.VMEM(DOSAGE_SHAPE, BF16), DMA],
+    [DMA((N,))],
 )
 associate = call(
     association_kernel,
@@ -390,7 +394,7 @@
     [(jax.ShapeDtypeStruct((CT, OWN, WIN), F32), VMEM)],
     [VMEM, HBM, VMEM],
     16,
-    [pltpu.VMEM(DOSAGE_SHAPE, BF16), pltpu.VMEM((N // 2, OWN * CT, LANES), F32), DMA],
+    [pltpu.VMEM(DOSAGE_SHAPE, BF16), pltpu.VMEM((N // 2, OWN * CT, LANES), F32), DMA((DONORS // PIECE,))],
 )
 
 
@@ -406,10 +410,9 @@
         keep(covariates),
     )
     parts = lax.all_to_all(parts, "cell", 0, 0, tiled=True)
-    (ordered,) = order_dosage(dosage)
     (library,) = sum_library(parts)
     library = lax.all_to_all(library, "gene", 0, 0, tiled=True)
-    (sent,) = sum_cells(parts)
+    sent, ordered = prepare(parts, dosage)
     (sent,) = express(keep(sent), library)
     sent = lax.all_to_all(sent, "donor", 0, 0, tiled=True)
     return associate(sent, keep(ordered), windows)[0]

time: 66.8 us -> 66.1 us (0.990)
  blocking collectives: 28.2 us -> 43.5 us
  starting transfers between devices: 14.9 us -> 6.83 us
  waiting for transfers between devices: 10.9 us -> 4.52 us
  Pallas kernels: 12.3 us -> 10.7 us
    all_to_all x0 -> x1, blocking collectives: none -> 15.4 us  [per_device(): sent = lax.all_to_all(sent, 'donor', 0, 0, tiled=True)]
    all_to_all x1 -> x0, starting transfers between devices: 8.05 us -> none  [per_device(): sent = lax.all_to_all(sent, 'donor', 0, 0, tiled=True)]
    all_to_all x1 -> x0, waiting for transfers between devices: 5.37 us -> none  [per_device(): sent = lax.all_to_all(sent, 'donor', 0, 0, tiled=True)]
    all_to_all x1, waiting for transfers between devices: 5.53 us -> 4.52 us  [per_device(): library = lax.all_to_all(library, 'gene', 0, 0, tiled=True)]
    pallas_call x2 -> x1, Pallas kernels: 3.52 us -> 2.53 us  [per_device(): sent, ordered = prepare(parts, dosage)]
  transfers between devices with their start and end apart: 2 -> 1, of which waited for: 2 -> 1; matrix products, arithmetic and copies ran while one was open for 0% -> 0% of each run, Pallas kernels for 5% -> 4%
where the time goes in v6:
time: 66.1 us; the launch traced here: 65.7 us
  blocking collectives  43.5 us (66%)
  Pallas kernels  10.7 us (16%)
  starting transfers between devices  6.83 us (10%)
  waiting for transfers between devices  4.52 us (7%)
    all_to_all x1, blocking collectives, per_device(): parts = lax.all_to_all(parts, 'cell', 0, 0, tiled=True)  28.1 us
    all_to_all x1, blocking collectives, per_device(): sent = lax.all_to_all(sent, 'donor', 0, 0, tiled=True)  15.4 us
    all_to_all x1, starting transfers between devices, per_device(): library = lax.all_to_all(library, 'gene', 0, 0, tiled=True)  6.83 us
    all_to_all x1, waiting for transfers between devices, per_device(): library = lax.all_to_all(library, 'gene', 0, 0, tiled=True)  4.52 us
    pallas_call x1, Pallas kernels, per_device(): return associate(sent, keep(ordered), windows)[0]  4.36 us
    pallas_call x1, Pallas kernels, per_device(): sent, ordered = prepare(parts, dosage)  2.53 us
    pallas_call x1, Pallas kernels, per_device(): pack(keep(counts), keep(cell_donor.reshape(CHUNKS, LANES)), keep(cell_typ...  1.7 us
  transfers between devices with their start and end apart: 1, of which 1 were waited for; matrix products, arithmetic and copies ran while one was open for 0% of the time, Pallas kernels for 4%

profile of v6, /device:TPU:1, one launch (start us, length us, event | category | flops | bytes accessed | tf_op | source)
XLA Modules:
  0.0 65.7 jit_solution(18226458975579883427)
XLA Ops:
  0.0 0.0 copy-start
  0.0 1.7 %pack.1 = f32[8,144,128]{2,1,0:T(8,128)S(1)} custom-call(s32[512,256]{1,0:T(8,128)} %counts_hbm.1, s32[4,128]{1,0:T(4,128)} %bitcast.2, s32[4,128]{1,0:T(4,128)} %bitcast.3, f32[8,50]{1,0:T(8,128)} %cov_hbm.1), custom_call_target="tpu_custom_call" | custom-call | tf_op jit(solution)/shard_map/pack/pallas_call | solution.py:406
  1.7 28.1 %all_to_all.15.part_ref = f32[8,144,128]{2,1,0:T(8,128)S(1)} all-to-all(f32[8,144,128]{2,1,0:T(8,128)S(1)} %pack.1), channel_id=1, replica_groups=mesh['cell'=8,'donor'=8,'gene'=8] {'cell'}, dimensions={0} | all-to-all | bytes 1179648 | tf_op jit(solution)/shard_map/all_to_all | solution.py:412
  29.8 1.1 %sum_library.1 = f32[8,3,4,128]{3,2,1,0:T(4,128)} custom-call(f32[8,144,128]{2,1,0:T(8,128)S(1)} %all_to_all.15.part_ref), custom_call_target="tpu_custom_call" | custom-call | tf_op jit(solution)/shard_map/sum_library/pallas_call | solution.py:413
  31.0 0.0 copy-start.1
  31.0 6.8 %all-to-all-start.1 = ((f32[8,3,4,128]{3,2,1,0:T(4,128)}), f32[8,3,4,128]{3,2,1,0:T(4,128)S(1)}, u32[]{:S(2)}, u32[]{:S(2)}) async-start(f32[8,3,4,128]{3,2,1,0:T(4,128)} %sum_library.1), calls=%async_computation.1 | async-start | bytes 98304 | tf_op jit(solution)/shard_map/all_to_all | solution.py:414
  37.8 0.0 copy-done
  37.8 2.5 %prepare.1 = (f32[8,80,128]{2,1,0:T(8,128)}, bf16[512,1024]{1,0:T(8,128)(2,1)}) custom-call(f32[8,144,128]{2,1,0:T(8,128)S(1)} %all_to_all.15.part_ref, s32[1024,512]{1,0:T(8,128)S(1)} %copy-done), custom_call_target="tpu_custom_call" | custom-call | tf_op jit(solution)/shard_map/prepare/pallas_call | solution.py:415
  40.3 4.5 %all-to-all-done.1.library_ref = f32[8,3,4,128]{3,2,1,0:T(4,128)S(1)} async-done(((f32[8,3,4,128]{3,2,1,0:T(4,128)}), f32[8,3,4,128]{3,2,1,0:T(4,128)S(1)}, u32[]{:S(2)}, u32[]{:S(2)}) %all-to-all-start.1) | async-done | bytes 49184 | tf_op jit(solution)/shard_map/all_to_all | solution.py:414
  44.9 1.0 %express.1 = f32[8,80,128]{2,1,0:T(8,128)S(1)} custom-call(f32[8,80,128]{2,1,0:T(8,128)} %get-tuple-element.7.sent_hbm, f32[8,3,4,128]{3,2,1,0:T(4,128)S(1)} %all-to-all-done.1.library_ref), custom_call_target="tpu_custom_call" | custom-call | tf_op jit(solution)/shard_map/express/pallas_call | solution.py:416
  45.9 15.4 %all_to_all.16.recv_ref = f32[8,80,128]{2,1,0:T(8,128)S(1)} all-to-all(f32[8,80,128]{2,1,0:T(8,128)S(1)} %express.1), channel_id=1, replica_groups=mesh['cell'=8,'donor'=8,'gene'=8] {'donor'}, dimensions={0} | all-to-all | bytes 655360 | tf_op jit(solution)/shard_map/all_to_all | solution.py:417
  61.3 0.0 copy-done.1
  61.3 4.4 %associate.1 = f32[24,4,1024]{2,1,0:T(4,128)} custom-call(f32[8,80,128]{2,1,0:T(8,128)S(1)} %all_to_all.16.recv_ref, bf16[512,1024]{1,0:T(8,128)(2,1)} %get-tuple-element.8.dosage_hbm, s32[4,1024]{1,0:T(4,128)S(1)} %copy-done.1), custom_call_target="tpu_custom_call" | custom-call | tf_op jit(solution)/shard_map/associate/pallas_call | solution.py:418
Async XLA Ops:
  0.0 37.8 %copy-start = (s32[1024,512]{1,0:T(8,128)S(1)}, s32[1024,512]{1,0:T(8,128)}, u32[]{:S(2)}) copy-start(s32[1024,512]{1,0:T(8,128)} %dosage_ref.1) | copy-start | bytes 6291460
  31.0 30.3 %copy-start.1 = (s32[4,1024]{1,0:T(4,128)S(1)}, s32[4,1024]{1,0:T(4,128)}, u32[]{:S(2)}) copy-start(s32[4,1024]{1,0:T(4,128)} %windows_ref.1) | copy-start | bytes 49156
  31.0 13.9 %all-to-all-start.1 = ((f32[8,3,4,128]{3,2,1,0:T(4,128)}), f32[8,3,4,128]{3,2,1,0:T(4,128)S(1)}, u32[]{:S(2)}, u32[]{:S(2)}) async-start(f32[8,3,4,128]{3,2,1,0:T(4,128)} %sum_library.1), calls=%async_computation.1 | async-start | bytes 98304 | tf_op jit(solution)/shard_map/all_to_all | solution.py:414

commit v7 on v6

--- a/solution.py
+++ b/solution.py
@@ -31,6 +31,7 @@
 WIN = 1024
 SPAN = 256
 PIECE = 64
+PANEL = 17
 DONOR_ROW = CHUNKS * GENE_PART
 TYPE_ROW = DONOR_ROW + CHUNKS
 TOTAL_ROW = TYPE_ROW + CHUNKS
@@ -127,7 +128,8 @@
 
 
 def prepare_kernel(
-    part_ref, dosage_ref, out_hbm, ordered_hbm, sum_ref, out_ref, ordered_ref, sems
+    part_ref, dosage_ref, out_hbm, design_hbm, ordered_hbm,
+    sum_ref, out_ref, design_ref, ordered_ref, sems,
 ):
     lane = lax.broadcasted_iota(I32, (SUB, LANES), 1)
     first_half = lax.broadcasted_iota(I32, (SUB, LANES), 0) < N // 2
@@ -138,9 +140,9 @@
         tiles.append(jnp.where(lane < NCOV, tile, jnp.where(lane == NCOV, 1.0, 0.0)))
     tiles.append(jnp.zeros((DON_GRP, LANES), F32))
     turned = jnp.concatenate(tiles, axis=0).T
-    design = turned[: DON_GRP // 2] + pltpu.roll(turned[DON_GRP // 2 : DON_GRP], DON_GRP, 1)
-    for peer in range(N):
-        out_ref[peer, EXPR_ROWS:, :] = design
+    design_ref[...] = turned[: DON_GRP // 2] + pltpu.roll(
+        turned[DON_GRP // 2 : DON_GRP], DON_GRP, 1
+    )
 
     def one_block(block):
         onehot, step = read_labels(part_ref, block)
@@ -172,6 +174,7 @@
         pltpu.make_async_copy(out_ref.at[peer], out_hbm.at[peer], sems.at[peer])
         for peer in range(N)
     ]
+    copies.append(pltpu.make_async_copy(design_ref, design_hbm, sems.at[N]))
     for copy in copies:
         copy.start()
     place = lax.broadcasted_iota(I32, (DONORS, 1), 0)
@@ -185,7 +188,7 @@
         ordered_ref[:, span] = moved.astype(BF16)
         copies.append(
             pltpu.make_async_copy(
-                ordered_ref.at[:, span], ordered_hbm.at[:, span], sems.at[N + index]
+                ordered_ref.at[:, span], ordered_hbm.at[:, span], sems.at[N + 1 + index]
             )
         )
         copies[-1].start()
@@ -193,11 +196,14 @@
         copy.wait()
 
 
-def expression_kernel(sent_hbm, library_ref, out_ref, sems):
+def expression_kernel(sent_hbm, design_hbm, library_ref, out_ref, design_ref, sems):
     arrivals = [
-        pltpu.make_async_copy(sent_hbm.at[peer], out_ref.at[peer], sems.at[peer])
+        pltpu.make_async_copy(
+            sent_hbm.at[peer], out_ref.at[peer, pl.ds(0, EXPR_ROWS)], sems.at[peer]
+        )
         for peer in range(N)
     ]
+    arrivals.append(pltpu.make_async_copy(design_hbm, design_ref, sems.at[N]))
     for copy in arrivals:
         copy.start()
     library = library_ref[0]
@@ -212,6 +218,9 @@
         ],
         axis=0,
     )
+    arrivals[N].wait()
+    for peer in range(N):
+        out_ref[peer, EXPR_ROWS:, :] = design_ref[...]
     for peer in range(N):
         arrivals[peer].wait()
         out_ref[peer, :EXPR_ROWS, :] += shift
@@ -270,18 +279,22 @@
     lane_id = lax.broadcasted_iota(I32, (rows, LANES), 1)
     row_col = lax.broadcasted_iota(I32, (rows, 1), 0)
     work = jnp.where(lane_id < 64, gram[:rows], jnp.where(lane_id - 64 == row_id, 1.0, 0.0))
-    for panel in range(0, ORDER, SUB):
-        members = range(panel, min(panel + SUB, ORDER))
+    for panel in range(0, ORDER, PANEL):
+        members = range(panel, min(panel + PANEL, ORDER))
+        base = panel // SUB * SUB
+        live, live_id = work[base:], row_id[base:]
         held = {
-            column: jnp.broadcast_to(work[:, column : column + 1], (rows, LANES))
+            column: jnp.broadcast_to(live[:, column : column + 1], live.shape)
             for column in members
         }
         for column in members:
             mine = held[column]
-            factor = jnp.where(row_id > column, mine, 0.0) * (1.0 / mine[column : column + 1])
+            spot = column - base
+            factor = jnp.where(live_id > column, mine, 0.0) * (1.0 / mine[spot : spot + 1])
             for later in range(column + 1, members.stop):
-                held[later] = held[later] - factor * mine[later : later + 1]
-            work = work - factor * work[column : column + 1]
+                held[later] = held[later] - factor * mine[later - base : later - base + 1]
+            live = live - factor * live[spot : spot + 1]
+        work = jnp.concatenate([work[:base], live], axis=0) if base else live
     pivots = jnp.sum(jnp.where(lane_id == row_id, work, 0.0), axis=1, keepdims=True)
     scale = 1.0 / jnp.sqrt(jnp.where(row_col < ORDER, pivots, 1.0))
     inverse = pltpu.roll(work, 64, 1)
@@ -341,6 +354,8 @@
 SUM_SHAPE = (SUM_ROWS, LANES)
 LIBRARY_SHAPE = (N, HALF // OWN, OWN, LANES)
 SEND_SHAPE = (N, SEND_ROWS, LANES)
+LOG_SHAPE = (N, EXPR_ROWS, LANES)
+DESIGN_SHAPE = (DON_GRP // 2, LANES)
 DOSAGE_SHAPE = (DONORS, SNPS)
 DMA = pltpu.SemaphoreType.DMA
 
@@ -370,23 +385,28 @@
 prepare = call(
     prepare_kernel,
     "prepare",
-    [(pltpu.HBM(SEND_SHAPE, F32), HBM), (pltpu.HBM(DOSAGE_SHAPE, BF16), HBM)],
+    [
+        (pltpu.HBM(LOG_SHAPE, F32), HBM),
+        (pltpu.HBM(DESIGN_SHAPE, F32), HBM),
+        (pltpu.HBM(DOSAGE_SHAPE, BF16), HBM),
+    ],
     [VMEM, VMEM],
     16,
     [
         pltpu.VMEM(SUM_SHAPE, F32),
-        pltpu.VMEM(SEND_SHAPE, F32),
+        pltpu.VMEM(LOG_SHAPE, F32),
+        pltpu.VMEM(DESIGN_SHAPE, F32),
         pltpu.VMEM(DOSAGE_SHAPE, BF16),
-        DMA((N + SNPS // SPAN,)),
+        DMA((N + 1 + SNPS // SPAN,)),
     ],
 )
 express = call(
     expression_kernel,
     "express",
     [(jax.ShapeDtypeStruct(SEND_SHAPE, F32), VMEM)],
-    [HBM, VMEM],
+    [HBM, HBM, VMEM],
     8,
-    [DMA((N,))],
+    [pltpu.VMEM(DESIGN_SHAPE, F32), DMA((N + 1,))],
 )
 associate = call(
     association_kernel,
@@ -412,8 +432,8 @@
     parts = lax.all_to_all(parts, "cell", 0, 0, tiled=True)
     (library,) = sum_library(parts)
     library = lax.all_to_all(library, "gene", 0, 0, tiled=True)
-    sent, ordered = prepare(parts, dosage)
-    (sent,) = express(keep(sent), library)
+    logs, design, ordered = prepare(parts, dosage)
+    (sent,) = express(keep(logs), keep(design), library)
     sent = lax.all_to_all(sent, "donor", 0, 0, tiled=True)
     return associate(sent, keep(ordered), windows)[0]
 

time: 66.1 us -> 65.6 us (level)
  no operation moved by 1% of the time
where the time goes in v7:
time: 65.6 us; the launch traced here: 65.2 us
  blocking collectives  43.5 us (66%)
  Pallas kernels  10.3 us (16%)
  starting transfers between devices  6.83 us (10%)
  waiting for transfers between devices  4.51 us (7%)
    all_to_all x1, blocking collectives, per_device(): parts = lax.all_to_all(parts, 'cell', 0, 0, tiled=True)  28.1 us
    all_to_all x1, blocking collectives, per_device(): sent = lax.all_to_all(sent, 'donor', 0, 0, tiled=True)  15.4 us
    all_to_all x1, starting transfers between devices, per_device(): library = lax.all_to_all(library, 'gene', 0, 0, tiled=True)  6.83 us
    all_to_all x1, waiting for transfers between devices, per_device(): library = lax.all_to_all(library, 'gene', 0, 0, tiled=True)  4.51 us
    pallas_call x1, Pallas kernels, per_device(): return associate(sent, keep(ordered), windows)[0]  3.95 us
    pallas_call x1, Pallas kernels, per_device(): logs, design, ordered = prepare(parts, dosage)  2.54 us
    pallas_call x1, Pallas kernels, per_device(): pack(keep(counts), keep(cell_donor.reshape(CHUNKS, LANES)), keep(cell_typ...  1.7 us
  transfers between devices with their start and end apart: 1, of which 1 were waited for; matrix products, arithmetic and copies ran while one was open for 0% of the time, Pallas kernels for 4%

profile of v7, /device:TPU:1, one launch (start us, length us, event | category | flops | bytes accessed | tf_op | source)
XLA Modules:
  0.0 65.2 jit_solution(1897405650331833461)
XLA Ops:
  0.0 0.0 copy-start
  0.0 1.7 %pack.1 = f32[8,144,128]{2,1,0:T(8,128)S(1)} custom-call(s32[512,256]{1,0:T(8,128)} %counts_hbm.1, s32[4,128]{1,0:T(4,128)} %bitcast.2, s32[4,128]{1,0:T(4,128)} %bitcast.3, f32[8,50]{1,0:T(8,128)} %cov_hbm.1), custom_call_target="tpu_custom_call" | custom-call | tf_op jit(solution)/shard_map/pack/pallas_call | solution.py:426
  1.7 28.1 %all_to_all.15.part_ref = f32[8,144,128]{2,1,0:T(8,128)S(1)} all-to-all(f32[8,144,128]{2,1,0:T(8,128)S(1)} %pack.1), channel_id=1, replica_groups=mesh['cell'=8,'donor'=8,'gene'=8] {'cell'}, dimensions={0} | all-to-all | bytes 1179648 | tf_op jit(solution)/shard_map/all_to_all | solution.py:432
  29.8 1.1 %sum_library.1 = f32[8,3,4,128]{3,2,1,0:T(4,128)} custom-call(f32[8,144,128]{2,1,0:T(8,128)S(1)} %all_to_all.15.part_ref), custom_call_target="tpu_custom_call" | custom-call | tf_op jit(solution)/shard_map/sum_library/pallas_call | solution.py:433
  31.0 0.0 copy-start.1
  31.0 6.8 %all-to-all-start.1 = ((f32[8,3,4,128]{3,2,1,0:T(4,128)}), f32[8,3,4,128]{3,2,1,0:T(4,128)S(1)}, u32[]{:S(2)}, u32[]{:S(2)}) async-start(f32[8,3,4,128]{3,2,1,0:T(4,128)} %sum_library.1), calls=%async_computation.1 | async-start | bytes 98304 | tf_op jit(solution)/shard_map/all_to_all | solution.py:434
  37.8 0.0 copy-done
  37.8 2.5 %prepare.1 = (f32[8,48,128]{2,1,0:T(8,128)}, f32[32,128]{1,0:T(8,128)}, bf16[512,1024]{1,0:T(8,128)(2,1)}) custom-call(f32[8,144,128]{2,1,0:T(8,128)S(1)} %all_to_all.15.part_ref, s32[1024,512]{1,0:T(8,128)S(1)} %copy-done), custom_call_target="tpu_custom_call" | custom-call | tf_op jit(solution)/shard_map/prepare/pallas_call | solution.py:435
  40.4 4.5 %all-to-all-done.1.library_ref = f32[8,3,4,128]{3,2,1,0:T(4,128)S(1)} async-done(((f32[8,3,4,128]{3,2,1,0:T(4,128)}), f32[8,3,4,128]{3,2,1,0:T(4,128)S(1)}, u32[]{:S(2)}, u32[]{:S(2)}) %all-to-all-start.1) | async-done | bytes 49184 | tf_op jit(solution)/shard_map/all_to_all | solution.py:434
  44.9 1.0 %express.1 = f32[8,80,128]{2,1,0:T(8,128)S(1)} custom-call(f32[8,48,128]{2,1,0:T(8,128)} %get-tuple-element.8.sent_hbm, f32[32,128]{1,0:T(8,128)} %get-tuple-element.9.design_hbm, f32[8,3,4,128]{3,2,1,0:T(4,128)S(1)} %all-to-all-done.1.library_ref), custom_call_target="tpu_custom_call" | custom-call | tf_op jit(solution)/shard_map/express/pallas_call | solution.py:436
  45.9 15.4 %all_to_all.16.recv_ref = f32[8,80,128]{2,1,0:T(8,128)S(1)} all-to-all(f32[8,80,128]{2,1,0:T(8,128)S(1)} %express.1), channel_id=1, replica_groups=mesh['cell'=8,'donor'=8,'gene'=8] {'donor'}, dimensions={0} | all-to-all | bytes 655360 | tf_op jit(solution)/shard_map/all_to_all | solution.py:437
  61.3 0.0 copy-done.1
  61.3 3.9 %associate.1 = f32[24,4,1024]{2,1,0:T(4,128)} custom-call(f32[8,80,128]{2,1,0:T(8,128)S(1)} %all_to_all.16.recv_ref, bf16[512,1024]{1,0:T(8,128)(2,1)} %get-tuple-element.10.dosage_hbm, s32[4,1024]{1,0:T(4,128)S(1)} %copy-done.1), custom_call_target="tpu_custom_call" | custom-call | tf_op jit(solution)/shard_map/associate/pallas_call | solution.py:438
Async XLA Ops:
  0.0 37.8 %copy-start = (s32[1024,512]{1,0:T(8,128)S(1)}, s32[1024,512]{1,0:T(8,128)}, u32[]{:S(2)}) copy-start(s32[1024,512]{1,0:T(8,128)} %dosage_ref.1) | copy-start | bytes 6291460
  31.0 30.3 %copy-start.1 = (s32[4,1024]{1,0:T(4,128)S(1)}, s32[4,1024]{1,0:T(4,128)}, u32[]{:S(2)}) copy-start(s32[4,1024]{1,0:T(4,128)} %windows_ref.1) | copy-start | bytes 49156
  31.0 13.9 %all-to-all-start.1 = ((f32[8,3,4,128]{3,2,1,0:T(4,128)}), f32[8,3,4,128]{3,2,1,0:T(4,128)S(1)}, u32[]{:S(2)}, u32[]{:S(2)}) async-start(f32[8,3,4,128]{3,2,1,0:T(4,128)} %sum_library.1), calls=%async_computation.1 | async-start | bytes 98304 | tf_op jit(solution)/shard_map/all_to_all | solution.py:434

commit v8 on v7

--- a/solution.py
+++ b/solution.py
@@ -29,7 +29,7 @@
 DONORS = N * DON_GRP
 SNPS = 1024
 WIN = 1024
-SPAN = 256
+SPAN = 512
 PIECE = 64
 PANEL = 17
 DONOR_ROW = CHUNKS * GENE_PART
@@ -102,7 +102,7 @@
 
 def library_kernel(part_ref, library_hbm, library_ref, sems):
     number = lax.broadcasted_iota(I32, (LIB_ROWS, CELLS), 0)
-    summed = jnp.zeros((2 * LIB_ROWS, LANES), F32)
+    lefts, onehots = [], []
     for block in range(N):
         onehot, step = read_labels(part_ref, block)
         total = part_ref[block, TOTAL_ROW:COV_ROW, :]
@@ -111,9 +111,14 @@
             [jnp.where(number == step, to_row(value), 0.0) for value in (high, total - high)],
             axis=0,
         )
-        summed = summed + lax.dot_general(
-            left.astype(BF16), onehot, NT, preferred_element_type=F32
-        )
+        lefts.append(left.astype(BF16))
+        onehots.append(onehot)
+    summed = lax.dot_general(
+        jnp.concatenate(lefts, axis=1),
+        jnp.concatenate(onehots, axis=1),
+        NT,
+        preferred_element_type=F32,
+    )
     summed = summed[:LIB_ROWS] + summed[LIB_ROWS:]
     for group in range(HALF // OWN):
         library_ref[group] = summed[group * OWN : (group + 1) * OWN]

time: 65.6 us -> 65.6 us (level)
  no operation moved by 1% of the time
where the time goes in v8:
time: 65.6 us; the launch traced here: 65.2 us
  blocking collectives  43.5 us (66%)
  Pallas kernels  10.3 us (16%)
  starting transfers between devices  6.83 us (10%)
  waiting for transfers between devices  4.52 us (7%)
    all_to_all x1, blocking collectives, per_device(): parts = lax.all_to_all(parts, 'cell', 0, 0, tiled=True)  28.1 us
    all_to_all x1, blocking collectives, per_device(): sent = lax.all_to_all(sent, 'donor', 0, 0, tiled=True)  15.4 us
    all_to_all x1, starting transfers between devices, per_device(): library = lax.all_to_all(library, 'gene', 0, 0, tiled=True)  6.83 us
    all_to_all x1, waiting for transfers between devices, per_device(): library = lax.all_to_all(library, 'gene', 0, 0, tiled=True)  4.52 us
    pallas_call x1, Pallas kernels, per_device(): return associate(sent, keep(ordered), windows)[0]  3.95 us
    pallas_call x1, Pallas kernels, per_device(): logs, design, ordered = prepare(parts, dosage)  2.52 us
    pallas_call x1, Pallas kernels, per_device(): pack(keep(counts), keep(cell_donor.reshape(CHUNKS, LANES)), keep(cell_typ...  1.7 us
  transfers between devices with their start and end apart: 1, of which 1 were waited for; matrix products, arithmetic and copies ran while one was open for 0% of the time, Pallas kernels for 4%

profile of v8, /device:TPU:1, one launch (start us, length us, event | category | flops | bytes accessed | tf_op | source)
XLA Modules:
  0.0 65.2 jit_solution(11079499713192619581)
XLA Ops:
  0.0 0.0 copy-start
  0.0 1.7 %pack.1 = f32[8,144,128]{2,1,0:T(8,128)S(1)} custom-call(s32[512,256]{1,0:T(8,128)} %counts_hbm.1, s32[4,128]{1,0:T(4,128)} %bitcast.2, s32[4,128]{1,0:T(4,128)} %bitcast.3, f32[8,50]{1,0:T(8,128)} %cov_hbm.1), custom_call_target="tpu_custom_call" | custom-call | tf_op jit(solution)/shard_map/pack/pallas_call | solution.py:431
  1.7 28.1 %all_to_all.15.part_ref = f32[8,144,128]{2,1,0:T(8,128)S(1)} all-to-all(f32[8,144,128]{2,1,0:T(8,128)S(1)} %pack.1), channel_id=1, replica_groups=mesh['cell'=8,'donor'=8,'gene'=8] {'cell'}, dimensions={0} | all-to-all | bytes 1179648 | tf_op jit(solution)/shard_map/all_to_all | solution.py:437
  29.8 1.1 %sum_library.1 = f32[8,3,4,128]{3,2,1,0:T(4,128)} custom-call(f32[8,144,128]{2,1,0:T(8,128)S(1)} %all_to_all.15.part_ref), custom_call_target="tpu_custom_call" | custom-call | tf_op jit(solution)/shard_map/sum_library/pallas_call | solution.py:438
  31.0 0.0 copy-start.1
  31.0 6.8 %all-to-all-start.1 = ((f32[8,3,4,128]{3,2,1,0:T(4,128)}), f32[8,3,4,128]{3,2,1,0:T(4,128)S(1)}, u32[]{:S(2)}, u32[]{:S(2)}) async-start(f32[8,3,4,128]{3,2,1,0:T(4,128)} %sum_library.1), calls=%async_computation.1 | async-start | bytes 98304 | tf_op jit(solution)/shard_map/all_to_all | solution.py:439
  37.8 0.0 copy-done
  37.8 2.5 %prepare.1 = (f32[8,48,128]{2,1,0:T(8,128)}, f32[32,128]{1,0:T(8,128)}, bf16[512,1024]{1,0:T(8,128)(2,1)}) custom-call(f32[8,144,128]{2,1,0:T(8,128)S(1)} %all_to_all.15.part_ref, s32[1024,512]{1,0:T(8,128)S(1)} %copy-done), custom_call_target="tpu_custom_call" | custom-call | tf_op jit(solution)/shard_map/prepare/pallas_call | solution.py:440
  40.3 4.5 %all-to-all-done.1.library_ref = f32[8,3,4,128]{3,2,1,0:T(4,128)S(1)} async-done(((f32[8,3,4,128]{3,2,1,0:T(4,128)}), f32[8,3,4,128]{3,2,1,0:T(4,128)S(1)}, u32[]{:S(2)}, u32[]{:S(2)}) %all-to-all-start.1) | async-done | bytes 49184 | tf_op jit(solution)/shard_map/all_to_all | solution.py:439
  44.9 1.0 %express.1 = f32[8,80,128]{2,1,0:T(8,128)S(1)} custom-call(f32[8,48,128]{2,1,0:T(8,128)} %get-tuple-element.8.sent_hbm, f32[32,128]{1,0:T(8,128)} %get-tuple-element.9.design_hbm, f32[8,3,4,128]{3,2,1,0:T(4,128)S(1)} %all-to-all-done.1.library_ref), custom_call_target="tpu_custom_call" | custom-call | tf_op jit(solution)/shard_map/express/pallas_call | solution.py:441
  45.9 15.4 %all_to_all.16.recv_ref = f32[8,80,128]{2,1,0:T(8,128)S(1)} all-to-all(f32[8,80,128]{2,1,0:T(8,128)S(1)} %express.1), channel_id=1, replica_groups=mesh['cell'=8,'donor'=8,'gene'=8] {'donor'}, dimensions={0} | all-to-all | bytes 655360 | tf_op jit(solution)/shard_map/all_to_all | solution.py:442
  61.3 0.0 copy-done.1
  61.3 3.9 %associate.1 = f32[24,4,1024]{2,1,0:T(4,128)} custom-call(f32[8,80,128]{2,1,0:T(8,128)S(1)} %all_to_all.16.recv_ref, bf16[512,1024]{1,0:T(8,128)(2,1)} %get-tuple-element.10.dosage_hbm, s32[4,1024]{1,0:T(4,128)S(1)} %copy-done.1), custom_call_target="tpu_custom_call" | custom-call | tf_op jit(solution)/shard_map/associate/pallas_call | solution.py:443
Async XLA Ops:
  0.0 37.8 %copy-start = (s32[1024,512]{1,0:T(8,128)S(1)}, s32[1024,512]{1,0:T(8,128)}, u32[]{:S(2)}) copy-start(s32[1024,512]{1,0:T(8,128)} %dosage_ref.1) | copy-start | bytes 6291460
  31.0 30.3 %copy-start.1 = (s32[4,1024]{1,0:T(4,128)S(1)}, s32[4,1024]{1,0:T(4,128)}, u32[]{:S(2)}) copy-start(s32[4,1024]{1,0:T(4,128)} %windows_ref.1) | copy-start | bytes 49156
  31.0 13.9 %all-to-all-start.1 = ((f32[8,3,4,128]{3,2,1,0:T(4,128)}), f32[8,3,4,128]{3,2,1,0:T(4,128)S(1)}, u32[]{:S(2)}, u32[]{:S(2)}) async-start(f32[8,3,4,128]{3,2,1,0:T(4,128)} %sum_library.1), calls=%async_computation.1 | async-start | bytes 98304 | tf_op jit(solution)/shard_map/all_to_all | solution.py:439

commit v9 on v8

--- a/solution.py
+++ b/solution.py
@@ -29,7 +29,7 @@
 DONORS = N * DON_GRP
 SNPS = 1024
 WIN = 1024
-SPAN = 512
+SPANS = ((0, 512), (512, 256), (768, 256))
 PIECE = 64
 PANEL = 17
 DONOR_ROW = CHUNKS * GENE_PART
@@ -186,8 +186,8 @@
     column = lax.broadcasted_iota(I32, (DONORS, DONORS), 1)
     source = (((place >> 3) & 7) << 6) + ((place >> 6) << 3) + (place & 7)
     order = jnp.where(column == source, 1.0, 0.0).astype(BF16)
-    for index in range(SNPS // SPAN):
-        span = pl.ds(index * SPAN, SPAN)
+    for index, (begin, size) in enumerate(SPANS):
+        span = pl.ds(begin, size)
         half = dosage_ref[span, :].astype(F32).astype(BF16)
         moved = lax.dot_general(order, half, NT, preferred_element_type=F32)
         ordered_ref[:, span] = moved.astype(BF16)
@@ -402,7 +402,7 @@
         pltpu.VMEM(LOG_SHAPE, F32),
         pltpu.VMEM(DESIGN_SHAPE, F32),
         pltpu.VMEM(DOSAGE_SHAPE, BF16),
-        DMA((N + 1 + SNPS // SPAN,)),
+        DMA((N + 1 + len(SPANS),)),
     ],
 )
 express = call(

time: 65.6 us -> 65.6 us (level)
  no operation moved by 1% of the time
where the time goes in v9:
time: 65.6 us; the launch traced here: 65.2 us
  blocking collectives  43.5 us (66%)
  Pallas kernels  10.2 us (16%)
  starting transfers between devices  6.83 us (10%)
  waiting for transfers between devices  4.57 us (7%)
    all_to_all x1, blocking collectives, per_device(): parts = lax.all_to_all(parts, 'cell', 0, 0, tiled=True)  28.1 us
    all_to_all x1, blocking collectives, per_device(): sent = lax.all_to_all(sent, 'donor', 0, 0, tiled=True)  15.4 us
    all_to_all x1, starting transfers between devices, per_device(): library = lax.all_to_all(library, 'gene', 0, 0, tiled=True)  6.83 us
    all_to_all x1, waiting for transfers between devices, per_device(): library = lax.all_to_all(library, 'gene', 0, 0, tiled=True)  4.57 us
    pallas_call x1, Pallas kernels, per_device(): return associate(sent, keep(ordered), windows)[0]  3.95 us
    pallas_call x1, Pallas kernels, per_device(): logs, design, ordered = prepare(parts, dosage)  2.48 us
    pallas_call x1, Pallas kernels, per_device(): pack(keep(counts), keep(cell_donor.reshape(CHUNKS, LANES)), keep(cell_typ...  1.7 us
  transfers between devices with their start and end apart: 1, of which 1 were waited for; matrix products, arithmetic and copies ran while one was open for 0% of the time, Pallas kernels for 4%

profile of v9, /device:TPU:1, one launch (start us, length us, event | category | flops | bytes accessed | tf_op | source)
XLA Modules:
  0.0 65.2 jit_solution(12015795960257466064)
XLA Ops:
  0.0 0.0 copy-start
  0.0 1.7 %pack.1 = f32[8,144,128]{2,1,0:T(8,128)S(1)} custom-call(s32[512,256]{1,0:T(8,128)} %counts_hbm.1, s32[4,128]{1,0:T(4,128)} %bitcast.2, s32[4,128]{1,0:T(4,128)} %bitcast.3, f32[8,50]{1,0:T(8,128)} %cov_hbm.1), custom_call_target="tpu_custom_call" | custom-call | tf_op jit(solution)/shard_map/pack/pallas_call | solution.py:431
  1.7 28.1 %all_to_all.15.part_ref = f32[8,144,128]{2,1,0:T(8,128)S(1)} all-to-all(f32[8,144,128]{2,1,0:T(8,128)S(1)} %pack.1), channel_id=1, replica_groups=mesh['cell'=8,'donor'=8,'gene'=8] {'cell'}, dimensions={0} | all-to-all | bytes 1179648 | tf_op jit(solution)/shard_map/all_to_all | solution.py:437
  29.8 1.1 %sum_library.1 = f32[8,3,4,128]{3,2,1,0:T(4,128)} custom-call(f32[8,144,128]{2,1,0:T(8,128)S(1)} %all_to_all.15.part_ref), custom_call_target="tpu_custom_call" | custom-call | tf_op jit(solution)/shard_map/sum_library/pallas_call | solution.py:438
  31.0 0.0 copy-start.1
  31.0 6.8 %all-to-all-start.1 = ((f32[8,3,4,128]{3,2,1,0:T(4,128)}), f32[8,3,4,128]{3,2,1,0:T(4,128)S(1)}, u32[]{:S(2)}, u32[]{:S(2)}) async-start(f32[8,3,4,128]{3,2,1,0:T(4,128)} %sum_library.1), calls=%async_computation.1 | async-start | bytes 98304 | tf_op jit(solution)/shard_map/all_to_all | solution.py:439
  37.8 0.0 copy-done
  37.8 2.5 %prepare.1 = (f32[8,48,128]{2,1,0:T(8,128)}, f32[32,128]{1,0:T(8,128)}, bf16[512,1024]{1,0:T(8,128)(2,1)}) custom-call(f32[8,144,128]{2,1,0:T(8,128)S(1)} %all_to_all.15.part_ref, s32[1024,512]{1,0:T(8,128)S(1)} %copy-done), custom_call_target="tpu_custom_call" | custom-call | tf_op jit(solution)/shard_map/prepare/pallas_call | solution.py:440
  40.3 4.6 %all-to-all-done.1.library_ref = f32[8,3,4,128]{3,2,1,0:T(4,128)S(1)} async-done(((f32[8,3,4,128]{3,2,1,0:T(4,128)}), f32[8,3,4,128]{3,2,1,0:T(4,128)S(1)}, u32[]{:S(2)}, u32[]{:S(2)}) %all-to-all-start.1) | async-done | bytes 49184 | tf_op jit(solution)/shard_map/all_to_all | solution.py:439
  44.9 1.0 %express.1 = f32[8,80,128]{2,1,0:T(8,128)S(1)} custom-call(f32[8,48,128]{2,1,0:T(8,128)} %get-tuple-element.8.sent_hbm, f32[32,128]{1,0:T(8,128)} %get-tuple-element.9.design_hbm, f32[8,3,4,128]{3,2,1,0:T(4,128)S(1)} %all-to-all-done.1.library_ref), custom_call_target="tpu_custom_call" | custom-call | tf_op jit(solution)/shard_map/express/pallas_call | solution.py:441
  45.9 15.4 %all_to_all.16.recv_ref = f32[8,80,128]{2,1,0:T(8,128)S(1)} all-to-all(f32[8,80,128]{2,1,0:T(8,128)S(1)} %express.1), channel_id=1, replica_groups=mesh['cell'=8,'donor'=8,'gene'=8] {'donor'}, dimensions={0} | all-to-all | bytes 655360 | tf_op jit(solution)/shard_map/all_to_all | solution.py:442
  61.3 0.0 copy-done.1
  61.3 3.9 %associate.1 = f32[24,4,1024]{2,1,0:T(4,128)} custom-call(f32[8,80,128]{2,1,0:T(8,128)S(1)} %all_to_all.16.recv_ref, bf16[512,1024]{1,0:T(8,128)(2,1)} %get-tuple-element.10.dosage_hbm, s32[4,1024]{1,0:T(4,128)S(1)} %copy-done.1), custom_call_target="tpu_custom_call" | custom-call | tf_op jit(solution)/shard_map/associate/pallas_call | solution.py:443
Async XLA Ops:
  0.0 37.8 %copy-start = (s32[1024,512]{1,0:T(8,128)S(1)}, s32[1024,512]{1,0:T(8,128)}, u32[]{:S(2)}) copy-start(s32[1024,512]{1,0:T(8,128)} %dosage_ref.1) | copy-start | bytes 6291460
  31.0 30.3 %copy-start.1 = (s32[4,1024]{1,0:T(4,128)S(1)}, s32[4,1024]{1,0:T(4,128)}, u32[]{:S(2)}) copy-start(s32[4,1024]{1,0:T(4,128)} %windows_ref.1) | copy-start | bytes 49156
  31.0 13.9 %all-to-all-start.1 = ((f32[8,3,4,128]{3,2,1,0:T(4,128)}), f32[8,3,4,128]{3,2,1,0:T(4,128)S(1)}, u32[]{:S(2)}, u32[]{:S(2)}) async-start(f32[8,3,4,128]{3,2,1,0:T(4,128)} %sum_library.1), calls=%async_computation.1 | async-start | bytes 98304 | tf_op jit(solution)/shard_map/all_to_all | solution.py:439
